TPU v7x, 128 devices: a whole 4x4x4 slice. The times are simulated.
128 devices in a mesh: clu: 32 (over z, x, core), row: 4 (over y).
Axes of the slice: x: 4, y: 4, z: 4, core: 2. Of those that a mesh axis runs over, the one named last changes fastest.
Arguments:
- embeddings: bfloat16 [524288, 1024], P(('clu', 'row')), may hold values from -8 to 8
- cluster_keys: int32 [524288], P(('clu', 'row')), may hold values from 0 to 127, as said below
- owner_map: int32 [128], replicated, may hold values from 0 to 127, as said below
- live_counts: int32 [128, 32], P(('clu', 'row')), may hold values from 0 to 128, as said below
- sub_centroids: bfloat16 [128, 256, 1024], P('clu'), may hold values from -6 to 6
Outputs:
- new_centroids: float32 [128, 256, 1024], P('clu', None, 'row')
- row_costs: float32 [524288], P(('clu', 'row'))
Inputs may be any that keep to these rules, and one draw needn't show every extreme that they name: For every live slot of block j, owner_map[cluster_keys] // 4 equals j. `owner_map`: A permutation of the cluster positions. `live_counts`: every device has a full block for some owner.
All inputs are finite; a program needn't handle non-finite values.
Results may differ from a plain program's by a relative error of at most 0.00098.
Values may be sent and summed in bfloat16 or wider, within the bound.
No kernel may reach another device: no remote copies, remote signals or barrier semaphores. Data moves between devices by JAX's collectives and lax.ppermute only.
A program may use at most 128 MiB of HBM per device.

v0:
```python
import jax
import jax.numpy as jnp
from jax import lax
from jax.sharding import PartitionSpec as P

inverse_temp = 1.0 / 32.0


def body(embeddings, cluster_keys, owner_map, live_counts, sub_centroids):
    owners = lax.axis_size("clu")
    groups = lax.axis_size("row")
    slots = embeddings.shape[0]
    features = embeddings.shape[1]
    capacity = slots // owners
    clusters_here = sub_centroids.shape[0]
    centers_each = sub_centroids.shape[1]
    table_size = owner_map.shape[0]
    slot_index = jnp.arange(slots, dtype=jnp.int32)
    block_index = slot_index // capacity
    owner_cols = jnp.arange(owners, dtype=jnp.int32)
    limit = jnp.sum(
        jnp.where(block_index[:, None] == owner_cols[None, :], live_counts[0][None, :], 0), axis=1
    )
    live = slot_index % capacity < limit
    table_cols = jnp.arange(table_size, dtype=jnp.int32)
    position = jnp.sum(
        jnp.where(cluster_keys[:, None] == table_cols[None, :], owner_map[None, :], 0), axis=1
    )
    local_code = jnp.where(live, position % clusters_here, -1)
    blocks = embeddings.reshape(owners, capacity, features)
    code_blocks = local_code.reshape(owners, capacity)
    received, codes_in = (
        lax.all_to_all(blocks, "clu", split_axis=0, concat_axis=0, tiled=True),
        lax.all_to_all(code_blocks, "clu", split_axis=0, concat_axis=0, tiled=True),
    )
    rows_in = received.reshape(slots, features)
    codes_flat = codes_in.reshape(slots)
    center_rows = sub_centroids.reshape(clusters_here * centers_each, features)
    squares_x = jnp.sum(rows_in.astype(jnp.float32) ** 2, axis=1)
    squares_c = jnp.sum(center_rows.astype(jnp.float32) ** 2, axis=1)
    products = lax.dot_general(
        rows_in, center_rows, (((1,), (1,)), ((), ())), preferred_element_type=jnp.float32
    )
    distance = (squares_x[:, None] - 2.0 * products + squares_c[None, :]).reshape(
        slots, clusters_here, centers_each
    )
    owned = (codes_flat[:, None] == jnp.arange(clusters_here, dtype=jnp.int32)[None, :]).astype(
        jnp.float32
    )
    probs = jax.nn.softmax(-distance * inverse_temp, axis=-1) * owned[:, :, None]
    costs = jnp.sum(probs * distance, axis=(1, 2)) / features
    counts_part = jnp.sum(probs, axis=0).reshape(-1)
    weights = probs.astype(jnp.bfloat16).reshape(slots, clusters_here * centers_each)
    partial_value = lax.dot_general(
        weights, rows_in, (((0,), (0,)), ((), ())), preferred_element_type=jnp.float32
    )
    share_width = features // groups
    share_start = lax.axis_index("row") * share_width
    counts_copies = jnp.broadcast_to(counts_part[:, None], (counts_part.shape[0], groups))
    summed, totals_cols = (
        lax.psum_scatter(partial_value, "row", scatter_dimension=1, tiled=True),
        lax.psum_scatter(counts_copies, "row", scatter_dimension=1, tiled=True),
    )
    totals = totals_cols[:, 0]
    old_share = lax.dynamic_slice_in_dim(center_rows, share_start, share_width, 1).astype(
        jnp.float32
    )
    updated = (summed + old_share) / (totals[:, None] + 1.0)
    new_centroids = updated.reshape(clusters_here, centers_each, share_width)
    returned = lax.all_to_all(
        costs.reshape(owners, capacity), "clu", split_axis=0, concat_axis=0, tiled=True
    )
    row_costs = returned.reshape(slots)
    return (new_centroids, row_costs)


def solution(mesh):
    return jax.shard_map(
        body,
        mesh=mesh,
        in_specs=(
            P(("clu", "row"), None),
            P(("clu", "row")),
            P(),
            P(("clu", "row"), None),
            P("clu", None, None),
        ),
        out_specs=(P("clu", None, "row"), P(("clu", "row"))),
        check_vma=False,
    )
```

profile of v0, /device:TPU:0, one launch (start us, length us, event | category | flops | bytes accessed | tf_op | source)
XLA Modules:
  0.0 246.3 jit_solution(7737762246411909343)
XLA Ops:
  7.2 0.0 copy-start
  7.2 1.0 select_reduce_fusion.1
  8.1 2.0 select_reduce_fusion
  10.1 0.1 compare_select_fusion.4
  10.2 15.4 %all_to_all.17 = s32[32,1,128]{2,1,0:T(1,128)S(1)} all-to-all(s32[32,1,128]{2,1,0:T(1,128)S(1)} %compare_select_fusion.4), channel_id=1, replica_groups=mesh['clu'=32,'row'=4] {'clu'}, dimensions={0} | all-to-all | bytes 32768 | tf_op jit(solution)/shard_map/all_to_all | solution.py:34
  25.6 5.0 %all-to-all-start = ((bf16[32,128,1024]{2,1,0:T(8,128)(2,1)}), bf16[32,128,1024]{2,1,0:T(8,128)(2,1)}, u32[]{:S(2)}, u32[]{:S(2)}) async-start(bf16[32,128,1024]{2,1,0:T(8,128)(2,1)} %bitcast.42), calls=%async_computation | async-start | bytes 16777216 | tf_op jit(solution)/shard_map/all_to_all | solution.py:33
  30.6 0.0 reduce-scatter.2.cloned.1.call-start
  30.6 0.0 copy-done
  30.6 0.5 multiply_reduce_fusion.2
  31.2 105.3 %all-to-all-done = bf16[32,128,1024]{2,1,0:T(8,128)(2,1)} async-done(((bf16[32,128,1024]{2,1,0:T(8,128)(2,1)}), bf16[32,128,1024]{2,1,0:T(8,128)(2,1)}, u32[]{:S(2)}, u32[]{:S(2)}) %all-to-all-start) | async-done | bytes 8388640 | tf_op jit(solution)/shard_map/all_to_all | solution.py:33
  136.5 5.1 %multiply_reduce_fusion.1 = f32[32,128]{1,0:T(8,128)S(1)} fusion(bf16[32,128,1024]{2,1,0:T(8,128)(2,1)} %all-to-all-done), kind=kLoop, calls=%fused_computation.11 | loop fusion | flops 12578816 | bytes 8404992 | tf_op jit(solution)/shard_map/reduce_sum | solution.py:39
  141.5 12.1 %bitcast_reduce_fusion = (f32[4096,4]{0,1:T(4,128)S(1)}, f32[4096,1024]{0,1:T(8,128)S(1)}) fusion(f32[1024]{0:T(1024)S(1)} %bitcast.53, f32[4096]{0:T(1024)S(1)} %bitcast.46, bf16[4096,1024]{1,0:T(8,128)(2,1)} %bitcast.2, bf16[1024,1024]{1,0:T(8,128)(2,1)S(1)} %bitcast.43), kind=kOutput, calls=%fused_computation.6 | convolution fusion | flops 8615084032 | bytes 27348992 | tf_op jit(solution)/shard_map/dot_general | solution.py:41
  153.7 9.6 %fusion = f32[4096,4,256]{0,2,1:T(8,128)} fusion(f32[4096,4]{0,1:T(4,128)S(1)} %get-tuple-element.5, f32[4096,1024]{0,1:T(8,128)S(1)} %get-tuple-element.6, f32[1024]{0:T(1024)S(1)} %bitcast.54, f32[4096]{0:T(1024)S(1)} %bitcast.47), kind=kOutput, calls=%fused_computation | output fusion | flops 25182464 | bytes 33640448 | tf_op jit(solution)/shard_map/div | solution.py:50
  163.3 14.0 %multiply_reduce_fusion = (f32[4096]{0:T(1024)S(1)}, f32[1024]{0:T(1024)S(1)}, bf16[4096,1024]{0,1:T(8,128)(2,1)}) fusion(f32[4096,1024]{0,1:T(8,128)S(1)} %get-tuple-element.6, f32[1024]{0:T(1024)S(1)} %bitcast.55, f32[4096]{0:T(1024)S(1)} %bitcast.48, f32[4096,4]{0,1:T(4,128)S(1)} %fusion.8, f32[4096,4,256]{0,2,1:T(8,128)} %fusion, ...), kind=kLoop, calls=%fused_computation.8 | loop fusion | flops 50326528 | bytes 42115072 | tf_op jit(solution)/shard_map/reduce_sum | solution.py:51
  177.3 0.0 copy-start.1
  177.3 15.0 %fusion.5 = f32[1024,1024]{1,0:T(8,128)} fusion(bf16[4096,1024]{1,0:T(8,128)(2,1)} %bitcast.2, bf16[4096,1024]{0,1:T(8,128)(2,1)} %get-tuple-element.4), kind=kOutput, calls=%fused_computation.13 | convolution fusion | flops 8589934592 | bytes 20971520 | tf_op jit(solution)/shard_map/dot_general | solution.py:54
  192.3 0.0 reduce-scatter.2.cloned.1.call-update
  192.3 0.0 copy-done.1
  192.3 0.6 dynamic-slice
  192.9 0.6 broadcast_multiply_fusion
  193.5 3.8 %all-to-all-start.2 = ((f32[32,1,128]{2,1,0:T(1,128)}), f32[32,1,128]{2,1,0:T(1,128)S(1)}, u32[]{:S(2)}, u32[]{:S(2)}) async-start(f32[32,1,128]{2,1,0:T(1,128)} %bitcast.14), calls=%async_computation.3 | async-start | bytes 32768 | tf_op jit(solution)/shard_map/all_to_all | solution.py:70
  197.4 17.8 %all-reduce = f32[1024,4]{0,1:T(4,128)S(1)} all-reduce(f32[1024,4]{0,1:T(4,128)S(1)} %broadcast_in_dim.52), channel_id=3, replica_groups=mesh['clu'=32,'row'=4] {'row'}, use_global_device_ids=true, to_apply=%region_8.9.clone | all-reduce | flops 4096 | bytes 32768
  215.2 0.7 dynamic-slice_add_fusion
  215.8 0.0 all-to-all-done.2
  215.8 20.6 %reduce-scatter.2.cloned.1.call-done = f32[1024,256]{1,0:T(8,128)} async-done(((f32[1024,1024]{1,0:T(8,128)}), f32[1024,256]{1,0:T(8,128)}) %reduce-scatter.2.cloned.1.call-update) | async-done | bytes 1048592 | tf_op jit(solution)/shard_map/reduce_scatter | solution.py:61
  236.5 2.4 add_divide_fusion
  238.9 0.6 copy.9
  (4 shorter events, 0.0 us)
Async XLA Ops:
  7.2 23.5 %copy-start = (bf16[4,256,1024]{2,1,0:T(8,128)(2,1)S(1)}, bf16[4,256,1024]{2,1,0:T(8,128)(2,1)}, u32[]{:S(2)}) copy-start(bf16[4,256,1024]{2,1,0:T(8,128)(2,1)} %param.9) | copy-start | bytes 6291460
  25.6 110.8 %all-to-all-start = ((bf16[32,128,1024]{2,1,0:T(8,128)(2,1)}), bf16[32,128,1024]{2,1,0:T(8,128)(2,1)}, u32[]{:S(2)}, u32[]{:S(2)}) async-start(bf16[32,128,1024]{2,1,0:T(8,128)(2,1)} %bitcast.42), calls=%async_computation | async-start | bytes 16777216 | tf_op jit(solution)/shard_map/all_to_all | solution.py:33
  30.6 205.9 %reduce-scatter.2.cloned.1.call-start = ((), (), s32[]{:S(2)}) async-start(), calls=%async_computation.4 | async-start | bytes 5242880 | tf_op jit(solution)/shard_map/reduce_scatter | solution.py:61
  177.3 15.1 %copy-start.1 = (u32[128]{0:T(128)S(1)}, u32[128]{0:T(128)}, u32[]{:S(2)}) copy-start(u32[128]{0:T(128)} %constant.72) | copy-start | bytes 1540
  193.5 22.3 %all-to-all-start.2 = ((f32[32,1,128]{2,1,0:T(1,128)}), f32[32,1,128]{2,1,0:T(1,128)S(1)}, u32[]{:S(2)}, u32[]{:S(2)}) async-start(f32[32,1,128]{2,1,0:T(1,128)} %bitcast.14), calls=%async_computation.3 | async-start | bytes 32768 | tf_op jit(solution)/shard_map/all_to_all | solution.py:70
Sparse Core Ops, SparseCore 0:
  192.4 43.9 reduce-scatter.1
where the time goes:
time: 248 us; the launch traced here: 246 us
  waiting for transfers between devices  126 us (51%)
  other arithmetic  35.8 us (14%)
  blocking collectives  33.2 us (13%)
  matrix products  27.2 us (11%)
  between operations  14.1 us (6%)
  starting transfers between devices  8.84 us (4%)
    all_to_all x1, waiting for transfers between devices, body(): lax.all_to_all(blocks, 'clu', split_axis=0, concat_axis=0, tiled=True)  105 us
    reduce_scatter x1, waiting for transfers between devices, body(): lax.psum_scatter(partial_value, 'row', scatter_dimension=1, tiled=True)  20.6 us
    unnamed x1, blocking collectives  17.8 us
    all_to_all x1, blocking collectives, body(): lax.all_to_all(code_blocks, 'clu', split_axis=0, concat_axis=0, tiled=True)  15.4 us
    dot_general x1, matrix products, body(): lax.dot_general(weights, rows_in, (((0,), (0,)), ((), ())), preferred_ele...  15 us
    reduce_sum x1, other arithmetic, body(): costs = jnp.sum(probs * distance, axis=(1, 2)) / features  14 us
    dot_general x1, matrix products, body(): lax.dot_general(rows_in, center_rows, (((1,), (1,)), ((), ())), preferred...  12.1 us
    div x1, other arithmetic, body(): jax.nn.softmax(-distance * inverse_temp, axis=-1) * owned[:, :, None]  9.59 us
  transfers between devices with their start and end apart: 3, of which 2 were waited for; matrix products, arithmetic and copies ran while one was open for 1% of the time, Pallas kernels for 0%

commit v1 on v0

v1 whole, which is shorter than its diff:
```python
import functools
import jax, jax.numpy as jnp
from jax import lax
from jax.experimental import pallas as pl
from jax.experimental.pallas import tpu as pltpu

inverse_temp = 1.0 / 32.0

def assign_kernel(tile, parts, first, last, *refs):
    it = iter(refs)
    y_ref = next(it) if last else None
    codes_ref, x_ref, c_ref, csq_ref = next(it), next(it), next(it), next(it)
    if not first:
        sums_in, counts_in = next(it), next(it)
    gain_ref = next(it)
    if last:
        own_ref, far = next(it), [next(it), next(it), next(it)]
        side_ref = next(it)
        sums, counts = next(it), next(it)
    else:
        sums, counts = next(it), next(it)
    step = pl.program_id(0)
    centers = c_ref.shape[0]
    clusters = 4
    each = centers // clusters

    @pl.when(step == 0)
    def _():
        if first:
            sums[...] = jnp.zeros_like(sums)
            counts[...] = jnp.zeros_like(counts)
        else:
            sums[...] = sums_in[...]
            counts[...] = counts_in[...]

    sub = tile // parts
    cc = c_ref[...]
    csq = csq_ref[...]
    prods = []
    for p in range(parts):
        prods.append(lax.dot_general(cc, x_ref[p * sub:(p + 1) * sub, :], (((1,), (1,)), ((), ())),
                                     preferred_element_type=jnp.float32))
    for p in range(parts):
        prod = prods[p]
        weights = [[] for _ in range(clusters)]
        tallies = [counts[c * each:(c + 1) * each, :] for c in range(clusters)]
        for j in range(sub // 128):
            lanes = slice(p * sub + j * 128, p * sub + (j + 1) * 128)
            code = codes_ref[0:1, lanes]
            pick = prod[0:each, j * 128:(j + 1) * 128] * (2.0 * inverse_temp) - csq[0:each, :]
            for c in range(1, clusters):
                other = prod[c * each:(c + 1) * each, j * 128:(j + 1) * 128] * (2.0 * inverse_temp) - csq[c * each:(c + 1) * each, :]
                pick = jnp.where(code == c, other, pick)
            top = jnp.max(pick, axis=0, keepdims=True)
            e = jnp.exp(pick - top)
            total = jnp.sum(e, axis=0, keepdims=True)
            inv = 1.0 / total
            gain_ref[0:1, lanes] = jnp.sum(e * pick, axis=0, keepdims=True) * inv * (-1.0 / inverse_temp)
            prob = e * inv
            for c in range(clusters):
                m = jnp.where(code == c, prob, 0.0)
                tallies[c] = tallies[c] + m
                weights[c].append(m.astype(jnp.bfloat16))
        for c in range(clusters):
            counts[c * each:(c + 1) * each, :] = tallies[c]
        w = jnp.concatenate([jnp.concatenate(ws, axis=1) for ws in weights], axis=0)
        sums[...] += jnp.dot(w, x_ref[p * sub:(p + 1) * sub, :], preferred_element_type=jnp.float32)

    if last:
        @pl.when(step == pl.num_programs(0) - 1)
        def _():
            y = y_ref[0]
            quarter = sums.shape[1] // 4
            own_ref[...] = sums[:, pl.ds(pl.multiple_of(y * quarter, quarter), quarter)]
            peak = jnp.max(jnp.abs(sums[...]), axis=1, keepdims=True)
            scale = jnp.maximum(peak, 1e-30) * (1.0 / 32766.0)
            inv = 1.0 / scale
            for k in range(1, 4):
                to = (y + k) % 4
                v = sums[:, pl.ds(pl.multiple_of(to * quarter, quarter), quarter)] * inv
                far[k - 1][...] = jnp.round(v).astype(jnp.int32).astype(jnp.int16)
            tot = jnp.sum(counts[...], axis=1, keepdims=True)
            col = lax.broadcasted_iota(jnp.int32, counts.shape, 1)
            both = jnp.where(col == 0, tot, jnp.where(col == 1, scale, 0.0))
            side_ref[...] = both.T[0:8, :]


def assign(rows, codes, centers, csq, carry=None, y=None, tile=512, parts=2):
    n, d = rows.shape
    m = centers.shape[0]
    first, last = carry is None, y is not None
    f32 = jnp.float32
    whole = lambda shape: pl.BlockSpec(shape, lambda i, *_: (0,) * len(shape))
    in_specs = [pl.BlockSpec((1, tile), lambda i, *_: (0, i)), pl.BlockSpec((tile, d), lambda i, *_: (i, 0)),
                whole((m, d)), whole((m, 1))]
    args = [codes, rows, centers, csq]
    if not first:
        in_specs += [whole((m, d)), whole((m, 128))]
        args += list(carry)
    out_specs = [pl.BlockSpec((1, tile), lambda i, *_: (0, i))]
    outs = [jax.ShapeDtypeStruct((1, n), f32)]
    scratch = []
    if last:
        out_specs += [whole((m, d // 4))] * 4 + [whole((8, m))]
        outs += [jax.ShapeDtypeStruct((m, d // 4), f32)] + [jax.ShapeDtypeStruct((m, d // 4), jnp.int16)] * 3 + [jax.ShapeDtypeStruct((8, m), f32)]
        scratch = [pltpu.VMEM((m, d), f32), pltpu.VMEM((m, 128), f32)]
        args = [y.reshape(1).astype(jnp.int32)] + args
    else:
        out_specs += [whole((m, d)), whole((m, 128))]
        outs += [jax.ShapeDtypeStruct((m, d), f32), jax.ShapeDtypeStruct((m, 128), f32)]
    return pl.pallas_call(
        functools.partial(assign_kernel, tile, parts, first, last),
        grid_spec=pltpu.PrefetchScalarGridSpec(num_scalar_prefetch=1 if last else 0, grid=(n // tile,), in_specs=in_specs,
            out_specs=out_specs, scratch_shapes=scratch),
        out_shape=outs,
        compiler_params=pltpu.CompilerParams(dimension_semantics=("arbitrary",), vmem_limit_bytes=56 * 1024 * 1024),
        cost_estimate=pl.CostEstimate(flops=4 * n * m * d, bytes_accessed=2 * n * d + 2 * m * d + 4 * m * d, transcendentals=n * m // 4),
    )(*args)


from jax.sharding import PartitionSpec as P

cuts = (0, 128)


def around(k, size):
    return [(i, (i + k) % size) for i in range(size)]


def body(embeddings, cluster_keys, owner_map, live_counts, sub_centroids):
    owners = lax.axis_size("clu")
    groups = lax.axis_size("row")
    slots, features = embeddings.shape
    capacity = slots // owners
    clusters_here, centers_each = sub_centroids.shape[:2]
    y = lax.axis_index("row").astype(jnp.int32)

    keys = cluster_keys.reshape(owners, capacity)
    table = jnp.arange(owner_map.shape[0], dtype=jnp.int32)
    position = jnp.sum(jnp.where(keys[:, :, None] == table, owner_map, 0), axis=2)
    live = jnp.arange(capacity, dtype=jnp.int32)[None, :] < live_counts[0][:, None]
    code_blocks = jnp.where(live, position % clusters_here, -1)
    codes_in = lax.all_to_all(code_blocks, "clu", split_axis=0, concat_axis=0, tiled=True)

    blocks = embeddings.reshape(owners, capacity, features)
    received = [
        lax.all_to_all(blocks[:, a:b], "clu", split_axis=0, concat_axis=0, tiled=True)
        for a, b in zip(cuts[:-1], cuts[1:])
    ]
    centers = sub_centroids.reshape(clusters_here * centers_each, features)
    center_squares = jnp.sum(centers.astype(jnp.float32) ** 2, axis=1, keepdims=True) * inverse_temp
    row_squares = jnp.sum(blocks.astype(jnp.float32) ** 2, axis=2)
    share = lax.dynamic_slice_in_dim(centers, y * (features // groups), features // groups, 1)

    carry = None
    gains = []
    for i, (a, b) in enumerate(zip(cuts[:-1], cuts[1:])):
        rows = received[i].reshape(owners * (b - a), features)
        codes = codes_in[:, a:b].reshape(1, owners * (b - a))
        end = b == capacity
        out = assign(rows, codes, centers, center_squares, carry, y if end else None, tiles[i], 2)
        gains.append(out[0].reshape(owners, b - a))
        carry = out[1:]
    own, far1, far2, far3, side = carry

    got2 = lax.ppermute(far2, "row", around(2, groups))
    got1 = lax.ppermute(far1, "row", around(1, groups))
    got3 = lax.ppermute(far3, "row", around(3, groups))
    sides = lax.all_gather(side[0:2], "row")
    returned = lax.all_to_all(jnp.concatenate(gains, axis=1), "clu", split_axis=0, concat_axis=0, tiled=True)

    total = jnp.sum(sides[:, 0], axis=0)
    summed = own + share.astype(jnp.float32)
    for k, got in ((1, got1), (2, got2), (3, got3)):
        scale = lax.dynamic_index_in_dim(sides, (y - k) % groups, 0, keepdims=False)[1]
        summed = summed + got.astype(jnp.float32) * scale[:, None]
    updated = summed / (total[:, None] + 1.0)
    new_centroids = updated.reshape(clusters_here, centers_each, features // groups)
    row_costs = jnp.where(live, row_squares + returned, 0.0) * (1.0 / features)
    return new_centroids, row_costs.reshape(slots)


tiles = (1024,)


def solution(mesh):
    return jax.shard_map(
        body,
        mesh=mesh,
        in_specs=(
            P(("clu", "row"), None),
            P(("clu", "row")),
            P(),
            P(("clu", "row"), None),
            P("clu", None, None),
        ),
        out_specs=(P("clu", None, "row"), P(("clu", "row"))),
        check_vma=False,
    )
```

time: 248 us -> 205 us (0.83)
  matrix products: 27.2 us -> 0 us
  Pallas kernels: 0 us -> 25.8 us
  other arithmetic: 35.8 us -> 11.9 us
  waiting for transfers between devices: 126 us -> 106 us
  between operations: 14.1 us -> 0.77 us
  starting transfers between devices: 8.84 us -> 17.1 us
  blocking collectives: 33.2 us -> 40 us
    dot_general x2 -> x0, matrix products: 27.2 us -> none  [the longest x1 15 us: body(): lax.dot_general(weights, rows_in, (((0,), (0,)), ((), ())), preferred_ele...]
    pallas_call x0 -> x1, Pallas kernels: none -> 25.8 us  [assign(): pl.pallas_call(functools.partial(assign_kernel, tile, parts, first, last)...]
    all_gather x0 -> x1, blocking collectives: none -> 24.7 us  [body(): sides = lax.all_gather(side[0:2], 'row')]
    reduce_scatter x1 -> x0, waiting for transfers between devices: 20.6 us -> none  [body(): lax.psum_scatter(partial_value, 'row', scatter_dimension=1, tiled=True)]
    unnamed x1 -> x0, blocking collectives: 17.8 us -> none
    reduce_sum x5 -> x4, other arithmetic: 22.5 us -> 7.58 us  [the longest x1 5.09 us: body(): row_squares = jnp.sum(blocks.astype(jnp.float32) ** 2, axis=2)]
    div x3 -> x1, other arithmetic: 12.6 us -> 2.85 us  [body(): updated = summed / (total[:, None] + 1.0)]
    ppermute x0 -> x3, starting transfers between devices: none -> 4.68 us  [the longest x1 3.07 us: body(): got3 = lax.ppermute(far3, 'row', around(3, groups))]
  transfers between devices with their start and end apart: 3 -> 5, of which waited for: 2 -> 2; matrix products, arithmetic and copies ran while one was open for 1% -> 4% of each run, Pallas kernels for 0% -> 0%
where the time goes in v1:
time: 205 us; the launch traced here: 204 us
  waiting for transfers between devices  106 us (52%)
  blocking collectives  40 us (20%)
  Pallas kernels  25.8 us (13%)
  starting transfers between devices  17.1 us (8%)
  other arithmetic  11.9 us (6%)
    all_to_all x1, waiting for transfers between devices, body(): lax.all_to_all(blocks[:, a:b], 'clu', split_axis=0, concat_axis=0, tiled=...  99.1 us
    pallas_call x1, Pallas kernels, assign(): pl.pallas_call(functools.partial(assign_kernel, tile, parts, first, last)...  25.8 us
    all_gather x1, blocking collectives, body(): sides = lax.all_gather(side[0:2], 'row')  24.7 us
    all_to_all x1, blocking collectives, body(): lax.all_to_all(code_blocks, 'clu', split_axis=0, concat_axis=0, tiled=True)  15.3 us
    all_to_all x1, starting transfers between devices, body(): lax.all_to_all(jnp.concatenate(gains, axis=1), 'clu', split_axis=0, conca...  7.34 us
    all_to_all x1, waiting for transfers between devices, body(): lax.all_to_all(jnp.concatenate(gains, axis=1), 'clu', split_axis=0, conca...  7.23 us
    all_to_all x1, starting transfers between devices, body(): lax.all_to_all(blocks[:, a:b], 'clu', split_axis=0, concat_axis=0, tiled=...  5.09 us
    reduce_sum x1, other arithmetic, body(): row_squares = jnp.sum(blocks.astype(jnp.float32) ** 2, axis=2)  5.09 us
  transfers between devices with their start and end apart: 5, of which 2 were waited for; matrix products, arithmetic and copies ran while one was open for 4% of the time, Pallas kernels for 0%

profile of v1, /device:TPU:0, one launch (start us, length us, event | category | flops | bytes accessed | tf_op | source)
XLA Modules:
  0.0 203.8 jit_solution(10278368764546582396)
XLA Ops:
  0.6 2.0 select_reduce_fusion
  2.6 0.7 fusion.1
  3.4 15.3 %all_to_all.23 = s32[32,1,128]{2,1,0:T(1,128)} all-to-all(s32[32,1,128]{2,1,0:T(1,128)S(1)} %bitcast.37), channel_id=1, replica_groups=mesh['clu'=32,'row'=4] {'clu'}, dimensions={0} | all-to-all | bytes 32768 | tf_op jit(solution)/shard_map/all_to_all | solution.py:143
  18.7 0.0 copy-start
  18.7 5.1 %all-to-all-start.1 = ((bf16[32,128,1024]{2,1,0:T(8,128)(2,1)}), bf16[32,128,1024]{2,1,0:T(8,128)(2,1)}, u32[]{:S(2)}, u32[]{:S(2)}) async-start(bf16[32,128,1024]{2,1,0:T(8,128)(2,1)} %bitcast.31), calls=%async_computation.1 | async-start | bytes 16777216 | tf_op jit(solution)/shard_map/all_to_all | solution.py:147
  23.9 0.0 copy-done
  23.9 0.5 multiply_reduce_fusion.1
  24.4 1.1 copy.14
  25.5 5.1 %multiply_reduce_fusion = f32[4096]{0:T(1024)S(1)} fusion(bf16[4096,1024]{1,0:T(8,128)(2,1)} %param.5), kind=kLoop, calls=%fused_computation | loop fusion | flops 12578816 | bytes 8404992 | tf_op jit(solution)/shard_map/reduce_sum | solution.py:152
  30.6 99.1 %all-to-all-done.1 = bf16[32,128,1024]{2,1,0:T(8,128)(2,1)} async-done(((bf16[32,128,1024]{2,1,0:T(8,128)(2,1)}), bf16[32,128,1024]{2,1,0:T(8,128)(2,1)}, u32[]{:S(2)}, u32[]{:S(2)}) %all-to-all-start.1) | async-done | bytes 8388640 | tf_op jit(solution)/shard_map/all_to_all | solution.py:147
  129.7 0.0 copy-start.1
  129.7 25.8 %shard_map.68 = (f32[1,4096]{1,0:T(1,128)}, f32[1024,256]{1,0:T(8,128)}, s16[1024,256]{1,0:T(8,128)(2,1)}, s16[1024,256]{1,0:T(8,128)(2,1)}, s16[1024,256]{1,0:T(8,128)(2,1)}, /*index=5*/f32[8,1024]{1,0:T(8,128)}) custom-call(s32[1]{0:T(128)} %bitcast.refs_0_, s32[1,4096]{1,0:T(1,128)} %bitcast.40, bf16[4096,1024]{1,0:T(8,128)(2,1)} %bitcast.7.refs_2_, ...), custom_call_target="tpu_custom_call" | custom-call | flops 17179869184 | bytes 14680064 | tf_op jit(solution)/shard_map/pallas_call | solution.py:111
  155.5 3.1 %collective-permute-start.2 = (s16[1024,256]{1,0:T(8,128)(2,1)}, s16[1024,256]{1,0:T(8,128)(2,1)S(1)}, u32[]{:S(2)}, u32[]{:S(2)}) collective-permute-start(s16[1024,256]{1,0:T(8,128)(2,1)} %get-tuple-element.12), channel_id=1, source_target_pairs={{0,3},{1,0},{2,1},{3,2},{4,7},{5,4},{6,5},{7,6},{8,11},{9,8},{10,9... | collective-permute-start | bytes 1572872 | tf_op jit(solution)/shard_map/ppermute | solution.py:168
  158.5 0.6 collective-permute-start.1
  159.1 1.0 collective-permute-start
  160.1 0.8 slice_bitcast_fusion
  160.9 24.7 %all-gather.1 = f32[4,2,1024]{2,1,0:T(2,128)S(1)} all-gather(f32[1,2,1024]{2,1,0:T(2,128)S(1)} %slice_bitcast_fusion), channel_id=2, replica_groups=mesh['clu'=32,'row'=4] {'row'}, dimensions={0}, use_global_device_ids=true | all-gather | bytes 40960 | tf_op jit(solution)/shard_map/all_gather | solution.py:169
  185.6 7.3 %all-to-all-start.2 = ((f32[32,1,128]{2,1,0:T(1,128)}), f32[32,1,128]{2,1,0:T(1,128)S(1)}, u32[]{:S(2)}, u32[]{:S(2)}) async-start(f32[32,1,128]{2,1,0:T(1,128)} %bitcast.41), calls=%async_computation.2 | async-start | bytes 32768 | tf_op jit(solution)/shard_map/all_to_all | solution.py:170
  193.0 7.2 %all-to-all-done.2 = f32[32,1,128]{2,1,0:T(1,128)S(1)} async-done(((f32[32,1,128]{2,1,0:T(1,128)}), f32[32,1,128]{2,1,0:T(1,128)S(1)}, u32[]{:S(2)}, u32[]{:S(2)}) %all-to-all-start.2) | async-done | bytes 16416 | tf_op jit(solution)/shard_map/all_to_all | solution.py:170
  200.2 0.0 copy-done.1
  200.2 0.7 select_multiply_fusion
  200.9 0.0 collective-permute-done.2
  200.9 0.0 collective-permute-done.1
  200.9 0.0 collective-permute-done
  200.9 2.9 %add_divide_fusion = f32[1024,256]{1,0:T(8,128)} fusion(s16[1024,256]{1,0:T(8,128)(2,1)S(1)} %collective-permute-done.2, s16[1024,256]{1,0:T(8,128)(2,1)S(1)} %collective-permute-done.1, s16[1024,256]{1,0:T(8,128)(2,1)S(1)} %collective-permute-done, f32[1024,256]{1,0:T(8,128)} %get-tuple-element.8, f32[1024]{0:T(1024)S(1)} %broadcast_add_fusion, ...), kind=kLoop, calls=%fused_computation.4 | loop fusion | flops 3145728 | bytes 4210692 | tf_op jit(solution)/shard_map/div | solution.py:177
  (5 shorter events, 0.1 us)
Async XLA Ops:
  18.7 5.2 %copy-start = (bf16[4,256,1024]{2,1,0:T(8,128)(2,1)S(1)}, bf16[4,256,1024]{2,1,0:T(8,128)(2,1)}, u32[]{:S(2)}) copy-start(bf16[4,256,1024]{2,1,0:T(8,128)(2,1)} %param.9) | copy-start | bytes 6291460
  18.7 111.0 %all-to-all-start.1 = ((bf16[32,128,1024]{2,1,0:T(8,128)(2,1)}), bf16[32,128,1024]{2,1,0:T(8,128)(2,1)}, u32[]{:S(2)}, u32[]{:S(2)}) async-start(bf16[32,128,1024]{2,1,0:T(8,128)(2,1)} %bitcast.31), calls=%async_computation.1 | async-start | bytes 16777216 | tf_op jit(solution)/shard_map/all_to_all | solution.py:147
  129.7 70.6 %copy-start.1 = (s32[1,32]{1,0:T(1,128)S(1)}, s32[1,32]{1,0:T(1,128)}, u32[]{:S(2)}) copy-start(s32[1,32]{1,0:T(1,128)} %param.8) | copy-start | bytes 388
  155.5 45.5 %collective-permute-start.2 = (s16[1024,256]{1,0:T(8,128)(2,1)}, s16[1024,256]{1,0:T(8,128)(2,1)S(1)}, u32[]{:S(2)}, u32[]{:S(2)}) collective-permute-start(s16[1024,256]{1,0:T(8,128)(2,1)} %get-tuple-element.12), channel_id=1, source_target_pairs={{0,3},{1,0},{2,1},{3,2},{4,7},{5,4},{6,5},{7,6},{8,11},{9,8},{10,9... | collective-permute-start | bytes 1572872 | tf_op jit(solution)/shard_map/ppermute | solution.py:168
  158.5 42.4 %collective-permute-start.1 = (s16[1024,256]{1,0:T(8,128)(2,1)}, s16[1024,256]{1,0:T(8,128)(2,1)S(1)}, u32[]{:S(2)}, u32[]{:S(2)}) collective-permute-start(s16[1024,256]{1,0:T(8,128)(2,1)} %get-tuple-element.11), channel_id=1, source_target_pairs={{0,2},{1,3},{2,0},{3,1},{4,6},{5,7},{6,4},{7,5},{8,10},{9,11},{10,... | collective-permute-start | bytes 1572872 | tf_op jit(solution)/shard_map/ppermute | solution.py:166
  159.1 41.8 %collective-permute-start = (s16[1024,256]{1,0:T(8,128)(2,1)}, s16[1024,256]{1,0:T(8,128)(2,1)S(1)}, u32[]{:S(2)}, u32[]{:S(2)}) collective-permute-start(s16[1024,256]{1,0:T(8,128)(2,1)} %get-tuple-element.9), channel_id=1, source_target_pairs={{0,1},{1,2},{2,3},{3,0},{4,5},{5,6},{6,7},{7,4},{8,9},{9,10},{10,1... | collective-permute-start | bytes 1572872 | tf_op jit(solution)/shard_map/ppermute | solution.py:167
  185.6 14.6 %all-to-all-start.2 = ((f32[32,1,128]{2,1,0:T(1,128)}), f32[32,1,128]{2,1,0:T(1,128)S(1)}, u32[]{:S(2)}, u32[]{:S(2)}) async-start(f32[32,1,128]{2,1,0:T(1,128)} %bitcast.41), calls=%async_computation.2 | async-start | bytes 32768 | tf_op jit(solution)/shard_map/all_to_all | solution.py:170

commit v2 on v1

--- a/solution.py
+++ b/solution.py
@@ -5,6 +5,14 @@
 from jax.experimental.pallas import tpu as pltpu
 
 inverse_temp = 1.0 / 32.0
+levels = 16.0
+most = 32700.0
+fine = 32000.0
+
+
+def step_of(level):
+    return jnp.exp2(level * (1.0 / levels)) * (1.0 / most)
+
 
 def assign_kernel(tile, parts, first, last, *refs):
     it = iter(refs)
@@ -15,7 +23,7 @@
     gain_ref = next(it)
     if last:
         own_ref, far = next(it), [next(it), next(it), next(it)]
-        side_ref = next(it)
+        home_ref = next(it)
         sums, counts = next(it), next(it)
     else:
         sums, counts = next(it), next(it)
@@ -73,16 +81,51 @@
             quarter = sums.shape[1] // 4
             own_ref[...] = sums[:, pl.ds(pl.multiple_of(y * quarter, quarter), quarter)]
             peak = jnp.max(jnp.abs(sums[...]), axis=1, keepdims=True)
-            scale = jnp.maximum(peak, 1e-30) * (1.0 / 32766.0)
-            inv = 1.0 / scale
+            level = jnp.ceil(jnp.log2(jnp.maximum(peak, 1e-30)) * levels)
+            inv = 1.0 / step_of(level)
             for k in range(1, 4):
                 to = (y + k) % 4
                 v = sums[:, pl.ds(pl.multiple_of(to * quarter, quarter), quarter)] * inv
-                far[k - 1][...] = jnp.round(v).astype(jnp.int32).astype(jnp.int16)
-            tot = jnp.sum(counts[...], axis=1, keepdims=True)
+                far[k - 1][0:centers, :] = jnp.round(v).astype(jnp.int32).astype(jnp.int16)
+            tot = jnp.sum(counts[...], axis=1, keepdims=True) * 4.0
+            high = jnp.floor(tot)
+            low = jnp.round((tot - high) * fine)
             col = lax.broadcasted_iota(jnp.int32, counts.shape, 1)
-            both = jnp.where(col == 0, tot, jnp.where(col == 1, scale, 0.0))
-            side_ref[...] = both.T[0:8, :]
+            notes = jnp.where(col == 0, high, jnp.where(col == 1, low, jnp.where(col == 2, level, 0.0)))
+            turned = notes.T[0:16, :].astype(jnp.int32).astype(jnp.int16)
+            for g in range(4):
+                part = turned[:, g * each:(g + 1) * each]
+                home_ref[g * 16:(g + 1) * 16, :] = part
+                for k in range(3):
+                    far[k][centers + g * 16:centers + (g + 1) * 16, :] = part
+
+
+def merge_kernel(own_ref, share_ref, home_ref, *refs):
+    far, out_ref = refs[:3], refs[3]
+    m = own_ref.shape[0]
+    each = m // 4
+    for g in range(4):
+        rows = slice(g * each, (g + 1) * each)
+        total = 1.0
+        summed = own_ref[rows, :] + share_ref[rows, :].astype(jnp.float32)
+        for k in range(4):
+            note = far[k - 1][m + g * 16:m + (g + 1) * 16, :] if k else home_ref[g * 16:(g + 1) * 16, :]
+            turned = jnp.concatenate([note.astype(jnp.int32).astype(jnp.float32)] * 8, axis=0).T
+            total = total + (turned[:, 0:1] + turned[:, 1:2] * (1.0 / fine)) * 0.25
+            if k:
+                summed = summed + far[k - 1][rows, :].astype(jnp.int32).astype(jnp.float32) * step_of(turned[:, 2:3])
+        out_ref[rows, :] = summed / total
+
+
+def merge(own, share, home, far):
+    space = pl.BlockSpec(memory_space=pltpu.VMEM)
+    return pl.pallas_call(
+        merge_kernel,
+        in_specs=[space] * 6,
+        out_specs=space,
+        out_shape=jax.ShapeDtypeStruct(own.shape, jnp.float32),
+        compiler_params=pltpu.CompilerParams(vmem_limit_bytes=24 * 1024 * 1024),
+    )(own, share, home, *far)
 
 
 def assign(rows, codes, centers, csq, carry=None, y=None, tile=512, parts=2):
@@ -101,8 +144,8 @@
     outs = [jax.ShapeDtypeStruct((1, n), f32)]
     scratch = []
     if last:
-        out_specs += [whole((m, d // 4))] * 4 + [whole((8, m))]
-        outs += [jax.ShapeDtypeStruct((m, d // 4), f32)] + [jax.ShapeDtypeStruct((m, d // 4), jnp.int16)] * 3 + [jax.ShapeDtypeStruct((8, m), f32)]
+        out_specs += [whole((m, d // 4))] + [whole((m + 64, d // 4))] * 3 + [whole((64, d // 4))]
+        outs += [jax.ShapeDtypeStruct((m, d // 4), f32)] + [jax.ShapeDtypeStruct((m + 64, d // 4), jnp.int16)] * 3 + [jax.ShapeDtypeStruct((64, d // 4), jnp.int16)]
         scratch = [pltpu.VMEM((m, d), f32), pltpu.VMEM((m, 128), f32)]
         args = [y.reshape(1).astype(jnp.int32)] + args
     else:
@@ -140,7 +183,9 @@
     position = jnp.sum(jnp.where(keys[:, :, None] == table, owner_map, 0), axis=2)
     live = jnp.arange(capacity, dtype=jnp.int32)[None, :] < live_counts[0][:, None]
     code_blocks = jnp.where(live, position % clusters_here, -1)
-    codes_in = lax.all_to_all(code_blocks, "clu", split_axis=0, concat_axis=0, tiled=True)
+    gathered = lax.all_gather(code_blocks.astype(jnp.int16), "clu")
+    me = lax.axis_index("clu")
+    codes_in = lax.dynamic_index_in_dim(gathered, me, 1, keepdims=False).astype(jnp.int32)
 
     blocks = embeddings.reshape(owners, capacity, features)
     received = [
@@ -150,8 +195,8 @@
     centers = sub_centroids.reshape(clusters_here * centers_each, features)
     center_squares = jnp.sum(centers.astype(jnp.float32) ** 2, axis=1, keepdims=True) * inverse_temp
     row_squares = jnp.sum(blocks.astype(jnp.float32) ** 2, axis=2)
+
     share = lax.dynamic_slice_in_dim(centers, y * (features // groups), features // groups, 1)
-
     carry = None
     gains = []
     for i, (a, b) in enumerate(zip(cuts[:-1], cuts[1:])):
@@ -161,20 +206,13 @@
         out = assign(rows, codes, centers, center_squares, carry, y if end else None, tiles[i], 2)
         gains.append(out[0].reshape(owners, b - a))
         carry = out[1:]
-    own, far1, far2, far3, side = carry
+    own, far1, far2, far3, home = carry
 
     got2 = lax.ppermute(far2, "row", around(2, groups))
     got1 = lax.ppermute(far1, "row", around(1, groups))
     got3 = lax.ppermute(far3, "row", around(3, groups))
-    sides = lax.all_gather(side[0:2], "row")
     returned = lax.all_to_all(jnp.concatenate(gains, axis=1), "clu", split_axis=0, concat_axis=0, tiled=True)
-
-    total = jnp.sum(sides[:, 0], axis=0)
-    summed = own + share.astype(jnp.float32)
-    for k, got in ((1, got1), (2, got2), (3, got3)):
-        scale = lax.dynamic_index_in_dim(sides, (y - k) % groups, 0, keepdims=False)[1]
-        summed = summed + got.astype(jnp.float32) * scale[:, None]
-    updated = summed / (total[:, None] + 1.0)
+    updated = merge(own, share, home, (got1, got2, got3))
     new_centroids = updated.reshape(clusters_here, centers_each, features // groups)
     row_costs = jnp.where(live, row_squares + returned, 0.0) * (1.0 / features)
     return new_centroids, row_costs.reshape(slots)

time: 205 us -> 189 us (0.922)
  waiting for transfers between devices: 106 us -> 10.3 us
  blocking collectives: 40 us -> 116 us
  other arithmetic: 11.9 us -> 8.24 us
  starting transfers between devices: 17.1 us -> 20.7 us
  Pallas kernels: 25.8 us -> 28.8 us
    all_to_all x1, waiting for transfers between devices: 99.1 us -> 0.01 us  [body(): lax.all_to_all(blocks[:, a:b], 'clu', split_axis=0, concat_axis=0, tiled=...]
    all_gather x1, blocking collectives: 24.7 us -> 116 us  [body(): gathered = lax.all_gather(code_blocks.astype(jnp.int16), 'clu')]
    all_to_all x1 -> x0, blocking collectives: 15.3 us -> none  [body(): lax.all_to_all(code_blocks, 'clu', split_axis=0, concat_axis=0, tiled=True)]
    ppermute x1, waiting for transfers between devices: 0.01 us -> 3.99 us  [body(): got2 = lax.ppermute(far2, 'row', around(2, groups))]
    all_to_all x1, starting transfers between devices: 5.09 us -> 8.52 us  [body(): lax.all_to_all(blocks[:, a:b], 'clu', split_axis=0, concat_axis=0, tiled=...]
    pallas_call x0 -> x1, Pallas kernels: none -> 2.86 us  [merge(): pl.pallas_call(merge_kernel, in_specs=[space] * 6, out_specs=space, out_s...]
    div x1 -> x0, other arithmetic: 2.85 us -> none  [body(): updated = summed / (total[:, None] + 1.0)]
    ppermute x1, starting transfers between devices: 0.62 us -> 2.9 us  [body(): got2 = lax.ppermute(far2, 'row', around(2, groups))]
  transfers between devices with their start and end apart: 5 -> 5, of which waited for: 2 -> 2; matrix products, arithmetic and copies ran while one was open for 4% -> 6% of each run, Pallas kernels for 0% -> 0%
where the time goes in v2:
time: 189 us; the launch traced here: 187 us
  blocking collectives  116 us (61%)
  Pallas kernels  28.8 us (15%)
  starting transfers between devices  20.7 us (11%)
  waiting for transfers between devices  10.3 us (5%)
  other arithmetic  8.24 us (4%)
  local copies, waits for them, and re-layouts  2.15 us (1%)
    all_gather x1, blocking collectives, body(): gathered = lax.all_gather(code_blocks.astype(jnp.int16), 'clu')  116 us
    pallas_call x1, Pallas kernels, assign(): pl.pallas_call(functools.partial(assign_kernel, tile, parts, first, last)...  26 us
    all_to_all x1, starting transfers between devices, body(): lax.all_to_all(blocks[:, a:b], 'clu', split_axis=0, concat_axis=0, tiled=...  8.52 us
    all_to_all x1, starting transfers between devices, body(): lax.all_to_all(jnp.concatenate(gains, axis=1), 'clu', split_axis=0, conca...  6.33 us
    all_to_all x1, waiting for transfers between devices, body(): lax.all_to_all(jnp.concatenate(gains, axis=1), 'clu', split_axis=0, conca...  6.26 us
    reduce_sum x1, other arithmetic, body(): row_squares = jnp.sum(blocks.astype(jnp.float32) ** 2, axis=2)  5.09 us
    ppermute x1, waiting for transfers between devices, body(): got2 = lax.ppermute(far2, 'row', around(2, groups))  3.99 us
  transfers between devices with their start and end apart: 5, of which 2 were waited for; matrix products, arithmetic and copies ran while one was open for 6% of the time, Pallas kernels for 0%

profile of v2, /device:TPU:0, one launch (start us, length us, event | category | flops | bytes accessed | tf_op | source)
XLA Modules:
  0.0 187.3 jit_solution(3218185548050793143)
XLA Ops:
  0.6 0.0 copy-start.2
  0.6 8.5 %all-to-all-start = ((bf16[32,128,1024]{2,1,0:T(8,128)(2,1)}), bf16[32,128,1024]{2,1,0:T(8,128)(2,1)}, u32[]{:S(2)}, u32[]{:S(2)}) async-start(bf16[32,128,1024]{2,1,0:T(8,128)(2,1)} %bitcast.27), calls=%async_computation | async-start | bytes 16777216 | tf_op jit(solution)/shard_map/all_to_all | solution.py:192
  9.2 0.0 copy-start.3
  9.2 0.0 copy-start.5
  9.2 0.0 copy-start.4
  9.2 0.0 copy-done.2
  9.2 0.5 multiply_reduce_fusion.1
  9.7 1.0 copy.13
  10.8 0.0 copy-done.3
  10.8 0.0 copy-done.5
  10.8 1.3 select_reduce_fusion
  12.0 0.0 copy-done.4
  12.1 0.1 fusion.2
  12.1 116.3 %all_gather.4 = s16[32,32,128]{2,1,0:T(8,128)(2,1)S(1)} all-gather(s16[1,32,128]{2,1,0:T(8,128)(2,1)S(1)} %fusion.2), channel_id=1, replica_groups=mesh['clu'=32,'row'=4] {'clu'}, dimensions={0}, use_global_device_ids=true | all-gather | bytes 270336 | tf_op jit(solution)/shard_map/all_gather | solution.py:186
  128.4 0.6 bitcast_convert_fusion.refs_1_
  129.1 0.0 all-to-all-done
  129.1 26.0 %shard_map.71 = (f32[1,4096]{1,0:T(1,128)}, f32[1024,256]{1,0:T(8,128)}, s16[1088,256]{1,0:T(8,128)(2,1)}, s16[1088,256]{1,0:T(8,128)(2,1)}, s16[1088,256]{1,0:T(8,128)(2,1)}, /*index=5*/s16[64,256]{1,0:T(8,128)(2,1)}) custom-call(s32[1]{0:T(128)} %bitcast.refs_0_, s32[1,4096]{1,0:T(1,128)} %bitcast_convert_fusion.refs_1_, ...), custom_call_target="tpu_custom_call" | custom-call | flops 17179869184 | bytes 14680064 | tf_op jit(solution)/shard_map/pallas_call | solution.py:154
  155.1 1.6 collective-permute-start
  156.7 2.9 %collective-permute-start.1 = (s16[1088,256]{1,0:T(8,128)(2,1)}, s16[1088,256]{1,0:T(8,128)(2,1)S(1)}, u32[]{:S(2)}, u32[]{:S(2)}) collective-permute-start(s16[1088,256]{1,0:T(8,128)(2,1)} %get-tuple-element.11), channel_id=1, source_target_pairs={{0,2},{1,3},{2,0},{3,1},{4,6},{5,7},{6,4},{7,5},{8,10},{9,11},{10,... | collective-permute-start | bytes 1671176 | tf_op jit(solution)/shard_map/ppermute | solution.py:211
  159.6 0.0 copy-start
  159.6 0.0 copy-start.1
  159.6 1.4 collective-permute-start.2
  161.0 5.1 %multiply_reduce_fusion = f32[4096]{0:T(1024)S(1)} fusion(bf16[4096,1024]{1,0:T(8,128)(2,1)} %param.5), kind=kLoop, calls=%fused_computation | loop fusion | flops 12578816 | bytes 8404992 | tf_op jit(solution)/shard_map/reduce_sum | solution.py:197
  166.1 6.3 %all-to-all-start.1 = ((f32[32,1,128]{2,1,0:T(1,128)}), f32[32,1,128]{2,1,0:T(1,128)S(1)}, u32[]{:S(2)}, u32[]{:S(2)}) async-start(f32[32,1,128]{2,1,0:T(1,128)} %bitcast.11), calls=%async_computation.1 | async-start | bytes 32768 | tf_op jit(solution)/shard_map/all_to_all | solution.py:214
  172.4 1.1 constant_dynamic-slice_fusion.share_ref
  173.5 6.3 %all-to-all-done.1 = f32[32,1,128]{2,1,0:T(1,128)S(1)} async-done(((f32[32,1,128]{2,1,0:T(1,128)}), f32[32,1,128]{2,1,0:T(1,128)S(1)}, u32[]{:S(2)}, u32[]{:S(2)}) %all-to-all-start.1) | async-done | bytes 16416 | tf_op jit(solution)/shard_map/all_to_all | solution.py:214
  179.7 0.7 select_multiply_fusion
  180.4 0.0 collective-permute-done.refs_0_
  180.4 4.0 %collective-permute-done.1.refs_1_ = s16[1088,256]{1,0:T(8,128)(2,1)S(1)} collective-permute-done((s16[1088,256]{1,0:T(8,128)(2,1)}, s16[1088,256]{1,0:T(8,128)(2,1)S(1)}, u32[]{:S(2)}, u32[]{:S(2)}) %collective-permute-start.1) | collective-permute-done | bytes 557088 | tf_op jit(solution)/shard_map/ppermute | solution.py:211
  184.4 0.0 collective-permute-done.2.refs_2_
  184.4 0.0 copy-done
  184.4 0.0 copy-done.1
  184.4 2.9 %shard_map.72 = f32[1024,256]{1,0:T(8,128)} custom-call(f32[1024,256]{1,0:T(8,128)S(1)} %copy-done, bf16[1024,256]{1,0:T(8,128)(2,1)S(1)} %constant_dynamic-slice_fusion.share_ref, s16[64,256]{1,0:T(8,128)(2,1)S(1)} %copy-done.1, s16[1088,256]{1,0:T(8,128)(2,1)S(1)} %collective-permute-done.refs_0_, s16[1088,256]{1,0:T(8,128)(2,1)S(1)} %collective-permute-done.1.refs_1_, ...), custom_call_target="tpu_custom_call" | custom-call | tf_op jit(solution)/shard_map/pallas_call | solution.py:122
  (2 shorter events, 0.0 us)
Async XLA Ops:
  0.6 8.6 %copy-start.2 = (bf16[4,256,1024]{2,1,0:T(8,128)(2,1)S(1)}, bf16[4,256,1024]{2,1,0:T(8,128)(2,1)}, u32[]{:S(2)}) copy-start(bf16[4,256,1024]{2,1,0:T(8,128)(2,1)} %param.9) | copy-start | bytes 6291460
  0.6 128.4 %all-to-all-start = ((bf16[32,128,1024]{2,1,0:T(8,128)(2,1)}), bf16[32,128,1024]{2,1,0:T(8,128)(2,1)}, u32[]{:S(2)}, u32[]{:S(2)}) async-start(bf16[32,128,1024]{2,1,0:T(8,128)(2,1)} %bitcast.27), calls=%async_computation | async-start | bytes 16777216 | tf_op jit(solution)/shard_map/all_to_all | solution.py:192
  9.2 1.6 copy-start.3
  9.2 1.6 copy-start.5
  9.2 2.9 %copy-start.4 = (s32[1,32]{1,0:T(1,128)S(1)}, s32[1,32]{1,0:T(1,128)}, u32[]{:S(2)}) copy-start(s32[1,32]{1,0:T(1,128)} %param.8) | copy-start | bytes 388
  155.1 25.4 %collective-permute-start = (s16[1088,256]{1,0:T(8,128)(2,1)}, s16[1088,256]{1,0:T(8,128)(2,1)S(1)}, u32[]{:S(2)}, u32[]{:S(2)}) collective-permute-start(s16[1088,256]{1,0:T(8,128)(2,1)} %get-tuple-element.10), channel_id=1, source_target_pairs={{0,1},{1,2},{2,3},{3,0},{4,5},{5,6},{6,7},{7,4},{8,9},{9,10},{10,1... | collective-permute-start | bytes 1671176 | tf_op jit(solution)/shard_map/ppermute | solution.py:212
  156.7 27.7 %collective-permute-start.1 = (s16[1088,256]{1,0:T(8,128)(2,1)}, s16[1088,256]{1,0:T(8,128)(2,1)S(1)}, u32[]{:S(2)}, u32[]{:S(2)}) collective-permute-start(s16[1088,256]{1,0:T(8,128)(2,1)} %get-tuple-element.11), channel_id=1, source_target_pairs={{0,2},{1,3},{2,0},{3,1},{4,6},{5,7},{6,4},{7,5},{8,10},{9,11},{10,... | collective-permute-start | bytes 1671176 | tf_op jit(solution)/shard_map/ppermute | solution.py:211
  159.6 24.8 %copy-start = (f32[1024,256]{1,0:T(8,128)S(1)}, f32[1024,256]{1,0:T(8,128)}, u32[]{:S(2)}) copy-start(f32[1024,256]{1,0:T(8,128)} %get-tuple-element.8.own_ref) | copy-start | bytes 3145732
  159.6 24.8 %copy-start.1 = (s16[64,256]{1,0:T(8,128)(2,1)S(1)}, s16[64,256]{1,0:T(8,128)(2,1)}, u32[]{:S(2)}) copy-start(s16[64,256]{1,0:T(8,128)(2,1)} %get-tuple-element.9.home_ref) | copy-start | bytes 98308
  159.6 24.8 %collective-permute-start.2 = (s16[1088,256]{1,0:T(8,128)(2,1)}, s16[1088,256]{1,0:T(8,128)(2,1)S(1)}, u32[]{:S(2)}, u32[]{:S(2)}) collective-permute-start(s16[1088,256]{1,0:T(8,128)(2,1)} %get-tuple-element.12), channel_id=1, source_target_pairs={{0,3},{1,0},{2,1},{3,2},{4,7},{5,4},{6,5},{7,6},{8,11},{9,8},{10,9... | collective-permute-start | bytes 1671176 | tf_op jit(solution)/shard_map/ppermute | solution.py:213
  166.1 13.7 %all-to-all-start.1 = ((f32[32,1,128]{2,1,0:T(1,128)}), f32[32,1,128]{2,1,0:T(1,128)S(1)}, u32[]{:S(2)}, u32[]{:S(2)}) async-start(f32[32,1,128]{2,1,0:T(1,128)} %bitcast.11), calls=%async_computation.1 | async-start | bytes 32768 | tf_op jit(solution)/shard_map/all_to_all | solution.py:214

commit v3 on v2

--- a/solution.py
+++ b/solution.py
@@ -24,7 +24,7 @@
     if last:
         own_ref, far = next(it), [next(it), next(it), next(it)]
         home_ref = next(it)
-        sums, counts = next(it), next(it)
+        sums, counts, arrived = next(it), next(it), next(it)
     else:
         sums, counts = next(it), next(it)
     step = pl.program_id(0)
@@ -38,8 +38,8 @@
             sums[...] = jnp.zeros_like(sums)
             counts[...] = jnp.zeros_like(counts)
         else:
-            sums[...] = sums_in[...]
-            counts[...] = counts_in[...]
+            pltpu.make_async_copy(sums_in, sums, arrived.at[0]).start()
+            pltpu.make_async_copy(counts_in, counts, arrived.at[1]).start()
 
     sub = tile // parts
     cc = c_ref[...]
@@ -48,6 +48,12 @@
     for p in range(parts):
         prods.append(lax.dot_general(cc, x_ref[p * sub:(p + 1) * sub, :], (((1,), (1,)), ((), ())),
                                      preferred_element_type=jnp.float32))
+    if not first:
+        @pl.when(step == 0)
+        def _():
+            pltpu.make_async_copy(counts_in, counts, arrived.at[1]).wait()
+            pltpu.make_async_copy(sums_in, sums, arrived.at[0]).wait()
+
     for p in range(parts):
         prod = prods[p]
         weights = [[] for _ in range(clusters)]
@@ -102,30 +108,71 @@
 
 def merge_kernel(own_ref, share_ref, home_ref, *refs):
     far, out_ref = refs[:3], refs[3]
-    m = own_ref.shape[0]
-    each = m // 4
-    for g in range(4):
-        rows = slice(g * each, (g + 1) * each)
-        total = 1.0
-        summed = own_ref[rows, :] + share_ref[rows, :].astype(jnp.float32)
-        for k in range(4):
-            note = far[k - 1][m + g * 16:m + (g + 1) * 16, :] if k else home_ref[g * 16:(g + 1) * 16, :]
-            turned = jnp.concatenate([note.astype(jnp.int32).astype(jnp.float32)] * 8, axis=0).T
-            total = total + (turned[:, 0:1] + turned[:, 1:2] * (1.0 / fine)) * 0.25
-            if k:
-                summed = summed + far[k - 1][rows, :].astype(jnp.int32).astype(jnp.float32) * step_of(turned[:, 2:3])
-        out_ref[rows, :] = summed / total
+    each = own_ref.shape[0]
+    m = 4 * each
+    g = pl.program_id(0)
+    rows = pl.ds(pl.multiple_of(g * each, each), each)
+    marks = pl.ds(pl.multiple_of(m + g * 16, 16), 16)
+    total = 1.0
+    summed = own_ref[...] + share_ref[...].astype(jnp.float32)
+    for k in range(4):
+        note = far[k - 1][marks, :] if k else home_ref[...]
+        turned = jnp.concatenate([note.astype(jnp.int32).astype(jnp.float32)] * 8, axis=0).T
+        total = total + (turned[:, 0:1] + turned[:, 1:2] * (1.0 / fine)) * 0.25
+        if k:
+            summed = summed + far[k - 1][rows, :].astype(jnp.int32).astype(jnp.float32) * step_of(turned[:, 2:3])
+    out_ref[...] = summed / total
 
 
 def merge(own, share, home, far):
-    space = pl.BlockSpec(memory_space=pltpu.VMEM)
+    m, quarter = own.shape
+    block = pl.BlockSpec((m // 4, quarter), lambda i: (i, 0))
     return pl.pallas_call(
         merge_kernel,
-        in_specs=[space] * 6,
-        out_specs=space,
+        grid=(4,),
+        in_specs=[block, block, pl.BlockSpec((16, quarter), lambda i: (i, 0))] + [pl.BlockSpec(memory_space=pltpu.VMEM)] * 3,
+        out_specs=block,
         out_shape=jax.ShapeDtypeStruct(own.shape, jnp.float32),
-        compiler_params=pltpu.CompilerParams(vmem_limit_bytes=24 * 1024 * 1024),
+        compiler_params=pltpu.CompilerParams(dimension_semantics=("arbitrary",), vmem_limit_bytes=24 * 1024 * 1024),
     )(own, share, home, *far)
+
+
+def pack_kernel(clusters, cut, keys_ref, map_ref, used_ref, x_ref, out_ref):
+    owners, capacity = keys_ref.shape
+    first = owners * pl.program_id(0)
+    table = jnp.broadcast_to(map_ref[...], (owners, capacity))
+    position = jnp.take_along_axis(table, keys_ref[...], axis=1)
+    used = jnp.broadcast_to(used_ref[...], (owners, used_ref.shape[1]))
+    mine = lax.broadcasted_iota(jnp.int32, used.shape, 1) == first + lax.broadcasted_iota(jnp.int32, used.shape, 0)
+    limit = jnp.sum(jnp.where(mine, used, 0), axis=1, keepdims=True)
+    live = lax.broadcasted_iota(jnp.int32, position.shape, 1) < limit
+    codes = jnp.where(live, lax.rem(position, clusters), -1)
+    edge = out_ref.shape[1] - 16
+    out_ref[:, 0:edge, :] = x_ref[:, 0:edge, :]
+    high = codes.astype(jnp.float32)
+    wide = jnp.concatenate([high] * (x_ref.shape[2] // capacity), axis=1)
+    row = lax.broadcasted_iota(jnp.int32, (16, x_ref.shape[2]), 0) + edge
+    for j in range(owners):
+        kept = x_ref[j, edge:edge + 16, :].astype(jnp.float32)
+        out_ref[j, edge:edge + 16, :] = jnp.where(row < cut, kept, wide[j:j + 1, :]).astype(jnp.bfloat16)
+
+
+def pack(blocks, keys, owner_map, used, clusters, cut, rows):
+    owners, capacity, features = blocks.shape
+    group = 8
+    return pl.pallas_call(
+        functools.partial(pack_kernel, clusters, cut),
+        grid=(owners // group,),
+        in_specs=[
+            pl.BlockSpec((group, capacity), lambda i: (i, 0)),
+            pl.BlockSpec((1, owner_map.shape[0]), lambda i: (0, 0)),
+            pl.BlockSpec((1, owners), lambda i: (0, 0)),
+            pl.BlockSpec((group, rows, features), lambda i: (i, 0, 0)),
+        ],
+        out_specs=pl.BlockSpec((group, rows, features), lambda i: (i, 0, 0)),
+        out_shape=jax.ShapeDtypeStruct((owners, rows, features), blocks.dtype),
+        compiler_params=pltpu.CompilerParams(dimension_semantics=("arbitrary",)),
+    )(keys, owner_map.reshape(1, -1), used, blocks)
 
 
 def assign(rows, codes, centers, csq, carry=None, y=None, tile=512, parts=2):
@@ -133,12 +180,13 @@
     m = centers.shape[0]
     first, last = carry is None, y is not None
     f32 = jnp.float32
+    resident = pl.BlockSpec(memory_space=pltpu.VMEM)
     whole = lambda shape: pl.BlockSpec(shape, lambda i, *_: (0,) * len(shape))
     in_specs = [pl.BlockSpec((1, tile), lambda i, *_: (0, i)), pl.BlockSpec((tile, d), lambda i, *_: (i, 0)),
-                whole((m, d)), whole((m, 1))]
+                resident, resident]
     args = [codes, rows, centers, csq]
     if not first:
-        in_specs += [whole((m, d)), whole((m, 128))]
+        in_specs += [pl.BlockSpec(memory_space=pl.ANY)] * 2
         args += list(carry)
     out_specs = [pl.BlockSpec((1, tile), lambda i, *_: (0, i))]
     outs = [jax.ShapeDtypeStruct((1, n), f32)]
@@ -146,7 +194,7 @@
     if last:
         out_specs += [whole((m, d // 4))] + [whole((m + 64, d // 4))] * 3 + [whole((64, d // 4))]
         outs += [jax.ShapeDtypeStruct((m, d // 4), f32)] + [jax.ShapeDtypeStruct((m + 64, d // 4), jnp.int16)] * 3 + [jax.ShapeDtypeStruct((64, d // 4), jnp.int16)]
-        scratch = [pltpu.VMEM((m, d), f32), pltpu.VMEM((m, 128), f32)]
+        scratch = [pltpu.VMEM((m, d), f32), pltpu.VMEM((m, 128), f32), pltpu.SemaphoreType.DMA((2,))]
         args = [y.reshape(1).astype(jnp.int32)] + args
     else:
         out_specs += [whole((m, d)), whole((m, 128))]
@@ -156,14 +204,16 @@
         grid_spec=pltpu.PrefetchScalarGridSpec(num_scalar_prefetch=1 if last else 0, grid=(n // tile,), in_specs=in_specs,
             out_specs=out_specs, scratch_shapes=scratch),
         out_shape=outs,
-        compiler_params=pltpu.CompilerParams(dimension_semantics=("arbitrary",), vmem_limit_bytes=56 * 1024 * 1024),
+        compiler_params=pltpu.CompilerParams(dimension_semantics=("arbitrary",), vmem_limit_bytes=60 * 1024 * 1024),
         cost_estimate=pl.CostEstimate(flops=4 * n * m * d, bytes_accessed=2 * n * d + 2 * m * d + 4 * m * d, transcendentals=n * m // 4),
     )(*args)
 
 
 from jax.sharding import PartitionSpec as P
 
-cuts = (0, 128)
+cut, extra = 88, 8
+tiles = (1024, 1280)
+parts = (2, 2)
 
 
 def around(k, size):
@@ -179,33 +229,33 @@
     y = lax.axis_index("row").astype(jnp.int32)
 
     keys = cluster_keys.reshape(owners, capacity)
-    table = jnp.arange(owner_map.shape[0], dtype=jnp.int32)
-    position = jnp.sum(jnp.where(keys[:, :, None] == table, owner_map, 0), axis=2)
-    live = jnp.arange(capacity, dtype=jnp.int32)[None, :] < live_counts[0][:, None]
-    code_blocks = jnp.where(live, position % clusters_here, -1)
-    gathered = lax.all_gather(code_blocks.astype(jnp.int16), "clu")
-    me = lax.axis_index("clu")
-    codes_in = lax.dynamic_index_in_dim(gathered, me, 1, keepdims=False).astype(jnp.int32)
-
     blocks = embeddings.reshape(owners, capacity, features)
-    received = [
-        lax.all_to_all(blocks[:, a:b], "clu", split_axis=0, concat_axis=0, tiled=True)
-        for a, b in zip(cuts[:-1], cuts[1:])
-    ]
     centers = sub_centroids.reshape(clusters_here * centers_each, features)
     center_squares = jnp.sum(centers.astype(jnp.float32) ** 2, axis=1, keepdims=True) * inverse_temp
     row_squares = jnp.sum(blocks.astype(jnp.float32) ** 2, axis=2)
-
     share = lax.dynamic_slice_in_dim(centers, y * (features // groups), features // groups, 1)
+
+    first = pack(blocks, keys, owner_map, live_counts, clusters_here, cut, cut + extra)
+    second = blocks[:, cut:]
+    second, center_squares, row_squares, share = lax.optimization_barrier(
+        (second, center_squares, row_squares, share)
+    )
+    received = [
+        lax.all_to_all(part, "clu", split_axis=0, concat_axis=0, tiled=True)
+        for part in (first, second)
+    ]
+    codes_in = received[0][:, cut, :capacity].astype(jnp.int32)
+    none = jnp.full((owners, extra), -1, jnp.int32)
+    codes = (jnp.concatenate([codes_in[:, :cut], none], axis=1), codes_in[:, cut:])
     carry = None
     gains = []
-    for i, (a, b) in enumerate(zip(cuts[:-1], cuts[1:])):
-        rows = received[i].reshape(owners * (b - a), features)
-        codes = codes_in[:, a:b].reshape(1, owners * (b - a))
-        end = b == capacity
-        out = assign(rows, codes, centers, center_squares, carry, y if end else None, tiles[i], 2)
-        gains.append(out[0].reshape(owners, b - a))
+    for i in range(2):
+        count = received[i].shape[1]
+        rows = received[i].reshape(owners * count, features)
+        out = assign(rows, codes[i].reshape(1, owners * count), centers, center_squares, carry, y if i else None, tiles[i], parts[i])
+        gains.append(out[0].reshape(owners, count))
         carry = out[1:]
+    gains[0] = gains[0][:, :cut]
     own, far1, far2, far3, home = carry
 
     got2 = lax.ppermute(far2, "row", around(2, groups))
@@ -214,11 +264,9 @@
     returned = lax.all_to_all(jnp.concatenate(gains, axis=1), "clu", split_axis=0, concat_axis=0, tiled=True)
     updated = merge(own, share, home, (got1, got2, got3))
     new_centroids = updated.reshape(clusters_here, centers_each, features // groups)
+    live = jnp.arange(capacity, dtype=jnp.int32)[None, :] < live_counts[0][:, None]
     row_costs = jnp.where(live, row_squares + returned, 0.0) * (1.0 / features)
     return new_centroids, row_costs.reshape(slots)
-
-
-tiles = (1024,)
 
 
 def solution(mesh):

time: 189 us -> 180 us (0.952)
  blocking collectives: 116 us -> 10.3 us
  waiting for transfers between devices: 10.3 us -> 88.7 us
  Pallas kernels: 28.8 us -> 41.9 us
  local copies, waits for them, and re-layouts: 2.15 us -> 10.4 us
  starting transfers between devices: 20.7 us -> 18.5 us
    all_gather x1 -> x0, blocking collectives: 116 us -> none  [body(): gathered = lax.all_gather(code_blocks.astype(jnp.int16), 'clu')]
    all_to_all x2, waiting for transfers between devices: 6.26 us -> 80.8 us  [body(): lax.all_to_all(part, 'clu', split_axis=0, concat_axis=0, tiled=True)]
    all_to_all x0 -> x1, blocking collectives: none -> 10.3 us  [body(): lax.all_to_all(jnp.concatenate(gains, axis=1), 'clu', split_axis=0, conca...]
    pallas_call x1 -> x2, Pallas kernels: 26 us -> 32.9 us  [assign(): pl.pallas_call(functools.partial(assign_kernel, tile, parts, first, last)...]
    pallas_call x1 -> x2, Pallas kernels: 2.86 us -> 8.96 us  [the longest x1 5.97 us: pack(): pl.pallas_call(functools.partial(pack_kernel, clusters, cut), grid=(owner...]
    ppermute x1, waiting for transfers between devices: 3.99 us -> 7.88 us  [body(): got2 = lax.ppermute(far2, 'row', around(2, groups))]
    slice x0 -> x2, local copies, waits for them, and re-layouts: none -> 3.7 us  [the longest x1 3.62 us: body(): second = blocks[:, cut:]]
    unnamed x14 -> x15, local copies, waits for them, and re-layouts: 1.07 us -> 3.51 us
  transfers between devices with their start and end apart: 5 -> 5, of which waited for: 2 -> 3; matrix products, arithmetic and copies ran while one was open for 6% -> 9% of each run, Pallas kernels for 0% -> 11%
where the time goes in v3:
time: 180 us; the launch traced here: 179 us
  waiting for transfers between devices  88.7 us (49%)
  Pallas kernels  41.9 us (23%)
  starting transfers between devices  18.5 us (10%)
  local copies, waits for them, and re-layouts  10.4 us (6%)
  blocking collectives  10.3 us (6%)
  other arithmetic  8.58 us (5%)
    all_to_all x2, waiting for transfers between devices, body(): lax.all_to_all(part, 'clu', split_axis=0, concat_axis=0, tiled=True)  80.8 us
    pallas_call x2, Pallas kernels, assign(): pl.pallas_call(functools.partial(assign_kernel, tile, parts, first, last)...  32.9 us
    all_to_all x2, starting transfers between devices, body(): lax.all_to_all(part, 'clu', split_axis=0, concat_axis=0, tiled=True)  12.6 us
    all_to_all x1, blocking collectives, body(): lax.all_to_all(jnp.concatenate(gains, axis=1), 'clu', split_axis=0, conca...  10.3 us
    ppermute x1, waiting for transfers between devices, body(): got2 = lax.ppermute(far2, 'row', around(2, groups))  7.88 us
    pallas_call x1, Pallas kernels, pack(): pl.pallas_call(functools.partial(pack_kernel, clusters, cut), grid=(owner...  5.97 us
    reduce_sum x1, other arithmetic, body(): row_squares = jnp.sum(blocks.astype(jnp.float32) ** 2, axis=2)  5.09 us
    slice x1, local copies, waits for them, and re-layouts, body(): second = blocks[:, cut:]  3.62 us
  transfers between devices with their start and end apart: 5, of which 3 were waited for; matrix products, arithmetic and copies ran while one was open for 9% of the time, Pallas kernels for 11%

profile of v3, /device:TPU:0, one launch (start us, length us, event | category | flops | bytes accessed | tf_op | source)
XLA Modules:
  0.0 179.0 jit_solution(439156057099878130)
XLA Ops:
  0.6 6.0 %shard_map.68 = bf16[32,96,1024]{2,1,0:T(8,128)(2,1)} custom-call(s32[32,128]{1,0:T(8,128)} %bitcast.34, s32[1,128]{1,0:T(1,128)} %bitcast.37, s32[1,32]{1,0:T(1,128)} %used_ref.1, bf16[32,128,1024]{2,1,0:T(8,128)(2,1)} %bitcast.21), custom_call_target="tpu_custom_call" | custom-call | tf_op jit(solution)/shard_map/pallas_call | solution.py:163
  6.6 8.4 %all-to-all-start = ((bf16[32,96,1024]{2,1,0:T(8,128)(2,1)}), bf16[32,96,1024]{2,1,0:T(8,128)(2,1)}, u32[]{:S(2)}, u32[]{:S(2)}) async-start(bf16[32,96,1024]{2,1,0:T(8,128)(2,1)} %shard_map.68), calls=%async_computation | async-start | bytes 12582912 | tf_op jit(solution)/shard_map/all_to_all | solution.py:244
  15.0 0.0 copy-start.2
  15.0 3.6 %slice.23 = bf16[32,40,1024]{2,1,0:T(8,128)(2,1)} slice(bf16[32,128,1024]{2,1,0:T(8,128)(2,1)} %bitcast.22), slice={[0:32], [88:128], [0:1024]} | slice | bytes 5242880 | tf_op jit(solution)/shard_map/slice | solution.py:239
  18.6 0.0 copy-done.2
  18.6 0.5 multiply_reduce_fusion.1
  19.1 0.1 constant_dynamic-slice_fusion.share_ref
  19.2 5.1 %multiply_reduce_fusion = f32[4096]{0:T(1024)S(1)} fusion(bf16[4096,1024]{1,0:T(8,128)(2,1)} %param.5), kind=kLoop, calls=%fused_computation | loop fusion | flops 12578816 | bytes 8404992 | tf_op jit(solution)/shard_map/reduce_sum | solution.py:235
  24.3 0.0 copy-start.6
  24.3 68.5 %all-to-all-done = bf16[32,96,1024]{2,1,0:T(8,128)(2,1)} async-done(((bf16[32,96,1024]{2,1,0:T(8,128)(2,1)}), bf16[32,96,1024]{2,1,0:T(8,128)(2,1)}, u32[]{:S(2)}, u32[]{:S(2)}) %all-to-all-start) | async-done | bytes 6291488 | tf_op jit(solution)/shard_map/all_to_all | solution.py:244
  92.8 4.2 %all-to-all-start.1 = ((bf16[32,40,1024]{2,1,0:T(8,128)(2,1)}), bf16[32,40,1024]{2,1,0:T(8,128)(2,1)S(1)}, u32[]{:S(2)}, u32[]{:S(2)}) async-start(bf16[32,40,1024]{2,1,0:T(8,128)(2,1)} %slice.23), calls=%async_computation.1 | async-start | bytes 5242880 | tf_op jit(solution)/shard_map/all_to_all | solution.py:244
  97.1 1.0 copy.10.refs_3_.refs_4_
  98.1 0.9 slice_convert_fusion
  99.0 0.1 slice.22
  99.1 0.7 reshape.68.refs_1_
  99.8 0.0 copy-done.6
  99.8 0.7 reshape.71.refs_0_
  100.4 20.3 %shard_map.69 = (f32[1,3072]{1,0:T(1,128)}, f32[1024,1024]{1,0:T(8,128)}, f32[1024,128]{1,0:T(8,128)}) custom-call(s32[1,3072]{1,0:T(1,128)} %reshape.71.refs_0_, bf16[3072,1024]{1,0:T(8,128)(2,1)} %bitcast.8.refs_1_, bf16[1024,1024]{1,0:T(8,128)(2,1)} %bitcast.23, f32[1024,1]{1,0:T(8,128)} %copy.10.refs_3_.refs_4_), custom_call_target="tpu_custom_call" | custom-call | flops 12884901888 | bytes 12582912 | tf_op jit(solution)/shard_map/pallas_call | solution.py:202
  120.7 12.3 %all-to-all-done.1 = bf16[32,40,1024]{2,1,0:T(8,128)(2,1)S(1)} async-done(((bf16[32,40,1024]{2,1,0:T(8,128)(2,1)}), bf16[32,40,1024]{2,1,0:T(8,128)(2,1)S(1)}, u32[]{:S(2)}, u32[]{:S(2)}) %all-to-all-start.1) | async-done | bytes 2621472 | tf_op jit(solution)/shard_map/all_to_all | solution.py:244
  133.0 0.0 copy-start.3
  133.0 1.5 copy-done.3
  134.5 0.0 copy-start.4
  134.5 0.0 copy-start.5
  134.5 12.6 %shard_map.70 = (f32[1,1280]{1,0:T(1,128)}, f32[1024,256]{1,0:T(8,128)}, s16[1088,256]{1,0:T(8,128)(2,1)}, s16[1088,256]{1,0:T(8,128)(2,1)}, s16[1088,256]{1,0:T(8,128)(2,1)}, /*index=5*/s16[64,256]{1,0:T(8,128)(2,1)}) custom-call(s32[1]{0:T(128)} %bitcast.refs_0_, s32[1,1280]{1,0:T(1,128)} %reshape.68.refs_1_, bf16[1280,1024]{1,0:T(8,128)(2,1)} %bitcast.26, ...), custom_call_target="tpu_custom_call" | custom-call | flops 5368709120 | bytes 8912896 | tf_op jit(solution)/shard_map/pallas_call | solution.py:202
  147.1 1.6 collective-permute-start
  148.8 2.9 %collective-permute-start.1 = (s16[1088,256]{1,0:T(8,128)(2,1)}, s16[1088,256]{1,0:T(8,128)(2,1)S(1)}, u32[]{:S(2)}, u32[]{:S(2)}) collective-permute-start(s16[1088,256]{1,0:T(8,128)(2,1)} %get-tuple-element.23), channel_id=1, source_target_pairs={{0,2},{1,3},{2,0},{3,1},{4,6},{5,7},{6,4},{7,5},{8,10},{9,11},{10,... | collective-permute-start | bytes 1671176 | tf_op jit(solution)/shard_map/ppermute | solution.py:261
  151.7 1.3 collective-permute-start.2
  153.0 0.7 reduce.3
  153.7 0.1 reshape.75
  153.8 0.5 broadcast.24
  154.3 0.0 copy-done.4
  154.3 0.7 reduce.6
  155.0 0.1 reshape.74
  155.1 0.1 pad_maximum_fusion
  155.2 10.3 %all_to_all.22 = f32[32,1,128]{2,1,0:T(1,128)S(1)} all-to-all(f32[32,1,128]{2,1,0:T(1,128)S(1)} %bitcast.32), channel_id=1, replica_groups=mesh['clu'=32,'row'=4] {'clu'}, dimensions={0} | all-to-all | bytes 32768 | tf_op jit(solution)/shard_map/all_to_all | solution.py:264
  165.5 0.0 copy-done.5
  165.5 0.7 multiply_bitcast_fusion
  166.2 0.0 collective-permute-done.refs_0_
  166.2 7.9 %collective-permute-done.1.refs_1_ = s16[1088,256]{1,0:T(8,128)(2,1)S(1)} collective-permute-done((s16[1088,256]{1,0:T(8,128)(2,1)}, s16[1088,256]{1,0:T(8,128)(2,1)S(1)}, u32[]{:S(2)}, u32[]{:S(2)}) %collective-permute-start.1) | collective-permute-done | bytes 557088 | tf_op jit(solution)/shard_map/ppermute | solution.py:261
  174.0 0.0 collective-permute-done.2.refs_2_
  174.1 0.0 copy-start
  174.1 1.2 copy-done
  175.3 0.0 copy-start.1
  175.3 0.8 copy-done.1
  176.0 3.0 %shard_map.71 = f32[1024,256]{1,0:T(8,128)} custom-call(f32[1024,256]{1,0:T(8,128)S(1)} %copy-done, bf16[1024,256]{1,0:T(8,128)(2,1)S(1)} %constant_dynamic-slice_fusion.share_ref, s16[64,256]{1,0:T(8,128)(2,1)S(1)} %copy-done.1, s16[1088,256]{1,0:T(8,128)(2,1)S(1)} %collective-permute-done.refs_0_, s16[1088,256]{1,0:T(8,128)(2,1)S(1)} %collective-permute-done.1.refs_1_, ...), custom_call_target="tpu_custom_call" | custom-call | tf_op jit(solution)/shard_map/pallas_call | solution.py:130
  (3 shorter events, 0.0 us)
Async XLA Ops:
  6.6 86.2 %all-to-all-start = ((bf16[32,96,1024]{2,1,0:T(8,128)(2,1)}), bf16[32,96,1024]{2,1,0:T(8,128)(2,1)}, u32[]{:S(2)}, u32[]{:S(2)}) async-start(bf16[32,96,1024]{2,1,0:T(8,128)(2,1)} %shard_map.68), calls=%async_computation | async-start | bytes 12582912 | tf_op jit(solution)/shard_map/all_to_all | solution.py:244
  15.0 3.6 %copy-start.2 = (bf16[4,256,1024]{2,1,0:T(8,128)(2,1)S(1)}, bf16[4,256,1024]{2,1,0:T(8,128)(2,1)}, u32[]{:S(2)}) copy-start(bf16[4,256,1024]{2,1,0:T(8,128)(2,1)} %param.9) | copy-start | bytes 6291460
  24.3 75.5 %copy-start.6 = (pred[96]{0:T(512)(128)(4,1)S(1)}, pred[96]{0:T(512)(128)(4,1)}, u32[]{:S(2)}) copy-start(pred[96]{0:T(512)(128)(4,1)} %constant.8.clone.1) | copy-start | bytes 292
  92.8 40.1 %all-to-all-start.1 = ((bf16[32,40,1024]{2,1,0:T(8,128)(2,1)}), bf16[32,40,1024]{2,1,0:T(8,128)(2,1)S(1)}, u32[]{:S(2)}, u32[]{:S(2)}) async-start(bf16[32,40,1024]{2,1,0:T(8,128)(2,1)} %slice.23), calls=%async_computation.1 | async-start | bytes 5242880 | tf_op jit(solution)/shard_map/all_to_all | solution.py:244
  133.0 1.5 copy-start.3
  134.5 19.9 %copy-start.4 = (f32[1,3072]{1,0:T(1,128)S(1)}, f32[1,3072]{1,0:T(1,128)}, u32[]{:S(2)}) copy-start(f32[1,3072]{1,0:T(1,128)} %get-tuple-element.26) | copy-start | bytes 36868
  134.5 31.0 %copy-start.5 = (s32[1,32]{1,0:T(1,128)S(1)}, s32[1,32]{1,0:T(1,128)}, u32[]{:S(2)}) copy-start(s32[1,32]{1,0:T(1,128)} %used_ref.1) | copy-start | bytes 388
  147.1 19.0 %collective-permute-start = (s16[1088,256]{1,0:T(8,128)(2,1)}, s16[1088,256]{1,0:T(8,128)(2,1)S(1)}, u32[]{:S(2)}, u32[]{:S(2)}) collective-permute-start(s16[1088,256]{1,0:T(8,128)(2,1)} %get-tuple-element.22), channel_id=1, source_target_pairs={{0,1},{1,2},{2,3},{3,0},{4,5},{5,6},{6,7},{7,4},{8,9},{9,10},{10,1... | collective-permute-start | bytes 1671176 | tf_op jit(solution)/shard_map/ppermute | solution.py:262
  148.8 25.3 %collective-permute-start.1 = (s16[1088,256]{1,0:T(8,128)(2,1)}, s16[1088,256]{1,0:T(8,128)(2,1)S(1)}, u32[]{:S(2)}, u32[]{:S(2)}) collective-permute-start(s16[1088,256]{1,0:T(8,128)(2,1)} %get-tuple-element.23), channel_id=1, source_target_pairs={{0,2},{1,3},{2,0},{3,1},{4,6},{5,7},{6,4},{7,5},{8,10},{9,11},{10,... | collective-permute-start | bytes 1671176 | tf_op jit(solution)/shard_map/ppermute | solution.py:261
  151.7 22.4 %collective-permute-start.2 = (s16[1088,256]{1,0:T(8,128)(2,1)}, s16[1088,256]{1,0:T(8,128)(2,1)S(1)}, u32[]{:S(2)}, u32[]{:S(2)}) collective-permute-start(s16[1088,256]{1,0:T(8,128)(2,1)} %get-tuple-element.24), channel_id=1, source_target_pairs={{0,3},{1,0},{2,1},{3,2},{4,7},{5,4},{6,5},{7,6},{8,11},{9,8},{10,9... | collective-permute-start | bytes 1671176 | tf_op jit(solution)/shard_map/ppermute | solution.py:263
  174.1 1.2 copy-start
  175.3 0.8 copy-start.1

commit v4 on v3

--- a/solution.py
+++ b/solution.py
@@ -106,7 +106,7 @@
                     far[k][centers + g * 16:centers + (g + 1) * 16, :] = part
 
 
-def merge_kernel(own_ref, share_ref, home_ref, *refs):
+def merge_kernel(own_ref, home_ref, *refs):
     far, out_ref = refs[:3], refs[3]
     each = own_ref.shape[0]
     m = 4 * each
@@ -114,27 +114,27 @@
     rows = pl.ds(pl.multiple_of(g * each, each), each)
     marks = pl.ds(pl.multiple_of(m + g * 16, 16), 16)
     total = 1.0
-    summed = own_ref[...] + share_ref[...].astype(jnp.float32)
+    summed = own_ref[...]
     for k in range(4):
-        note = far[k - 1][marks, :] if k else home_ref[...]
-        turned = jnp.concatenate([note.astype(jnp.int32).astype(jnp.float32)] * 8, axis=0).T
+        note = far[k - 1][marks, :].astype(jnp.int32).astype(jnp.float32) if k else home_ref[...]
+        turned = jnp.concatenate([note] * 8, axis=0).T
         total = total + (turned[:, 0:1] + turned[:, 1:2] * (1.0 / fine)) * 0.25
         if k:
             summed = summed + far[k - 1][rows, :].astype(jnp.int32).astype(jnp.float32) * step_of(turned[:, 2:3])
     out_ref[...] = summed / total
 
 
-def merge(own, share, home, far):
+def merge(own, home, far):
     m, quarter = own.shape
     block = pl.BlockSpec((m // 4, quarter), lambda i: (i, 0))
     return pl.pallas_call(
         merge_kernel,
         grid=(4,),
-        in_specs=[block, block, pl.BlockSpec((16, quarter), lambda i: (i, 0))] + [pl.BlockSpec(memory_space=pltpu.VMEM)] * 3,
+        in_specs=[block, pl.BlockSpec((16, quarter), lambda i: (i, 0))] + [pl.BlockSpec(memory_space=pltpu.VMEM)] * 3,
         out_specs=block,
         out_shape=jax.ShapeDtypeStruct(own.shape, jnp.float32),
         compiler_params=pltpu.CompilerParams(dimension_semantics=("arbitrary",), vmem_limit_bytes=24 * 1024 * 1024),
-    )(own, share, home, *far)
+    )(own, home, *far)
 
 
 def pack_kernel(clusters, cut, keys_ref, map_ref, used_ref, x_ref, out_ref):
@@ -213,7 +213,7 @@
 
 cut, extra = 88, 8
 tiles = (1024, 1280)
-parts = (2, 2)
+parts = (2, 1)
 
 
 def around(k, size):
@@ -262,7 +262,7 @@
     got1 = lax.ppermute(far1, "row", around(1, groups))
     got3 = lax.ppermute(far3, "row", around(3, groups))
     returned = lax.all_to_all(jnp.concatenate(gains, axis=1), "clu", split_axis=0, concat_axis=0, tiled=True)
-    updated = merge(own, share, home, (got1, got2, got3))
+    updated = merge(own + share.astype(jnp.float32), home.astype(jnp.float32), (got1, got2, got3))
     new_centroids = updated.reshape(clusters_here, centers_each, features // groups)
     live = jnp.arange(capacity, dtype=jnp.int32)[None, :] < live_counts[0][:, None]
     row_costs = jnp.where(live, row_squares + returned, 0.0) * (1.0 / features)

time: 180 us -> 176 us (0.978)
  blocking collectives: 10.3 us -> 0 us
  starting transfers between devices: 18.5 us -> 22.3 us
  waiting for transfers between devices: 88.7 us -> 92.4 us
  other arithmetic: 8.58 us -> 11.3 us
  local copies, waits for them, and re-layouts: 10.4 us -> 8.37 us
    all_to_all x1 -> x0, blocking collectives: 10.3 us -> none  [body(): lax.all_to_all(jnp.concatenate(gains, axis=1), 'clu', split_axis=0, conca...]
    all_to_all x0 -> x1, waiting for transfers between devices: none -> 5.17 us  [body(): lax.all_to_all(jnp.concatenate(gains, axis=1), 'clu', split_axis=0, conca...]
    all_to_all x0 -> x1, starting transfers between devices: none -> 3.83 us  [body(): lax.all_to_all(jnp.concatenate(gains, axis=1), 'clu', split_axis=0, conca...]
    unnamed x15 -> x11, local copies, waits for them, and re-layouts: 3.51 us -> 1.52 us
  transfers between devices with their start and end apart: 5 -> 6, of which waited for: 3 -> 4; matrix products, arithmetic and copies ran while one was open for 9% -> 10% of each run, Pallas kernels for 11% -> 12%
where the time goes in v4:
time: 176 us
  waiting for transfers between devices  92.4 us (52%)
  Pallas kernels  40.8 us (23%)
  starting transfers between devices  22.3 us (13%)
  other arithmetic  11.3 us (6%)
  local copies, waits for them, and re-layouts  8.37 us (5%)
    all_to_all x2, waiting for transfers between devices, body(): lax.all_to_all(part, 'clu', split_axis=0, concat_axis=0, tiled=True)  80.8 us
    pallas_call x2, Pallas kernels, assign(): pl.pallas_call(functools.partial(assign_kernel, tile, parts, first, last)...  31.8 us
    all_to_all x2, starting transfers between devices, body(): lax.all_to_all(part, 'clu', split_axis=0, concat_axis=0, tiled=True)  12.6 us
    ppermute x1, waiting for transfers between devices, body(): got2 = lax.ppermute(far2, 'row', around(2, groups))  6.46 us
    pallas_call x1, Pallas kernels, pack(): pl.pallas_call(functools.partial(pack_kernel, clusters, cut), grid=(owner...  5.97 us
    all_to_all x1, waiting for transfers between devices, body(): lax.all_to_all(jnp.concatenate(gains, axis=1), 'clu', split_axis=0, conca...  5.17 us
    reduce_sum x1, other arithmetic, body(): row_squares = jnp.sum(blocks.astype(jnp.float32) ** 2, axis=2)  5.09 us
    all_to_all x1, starting transfers between devices, body(): lax.all_to_all(jnp.concatenate(gains, axis=1), 'clu', split_axis=0, conca...  3.83 us
  transfers between devices with their start and end apart: 6, of which 4 were waited for; matrix products, arithmetic and copies ran while one was open for 10% of the time, Pallas kernels for 12%

profile of v4, /device:TPU:0, one launch (start us, length us, event | category | flops | bytes accessed | tf_op | source)
XLA Modules:
  0.0 175.9 jit_solution(11709843287259246570)
XLA Ops:
  0.6 6.0 %shard_map.68 = bf16[32,96,1024]{2,1,0:T(8,128)(2,1)} custom-call(s32[32,128]{1,0:T(8,128)} %bitcast.33, s32[1,128]{1,0:T(1,128)} %bitcast.36, s32[1,32]{1,0:T(1,128)} %used_ref.1, bf16[32,128,1024]{2,1,0:T(8,128)(2,1)} %bitcast.21), custom_call_target="tpu_custom_call" | custom-call | tf_op jit(solution)/shard_map/pallas_call | solution.py:163
  6.6 8.4 %all-to-all-start = ((bf16[32,96,1024]{2,1,0:T(8,128)(2,1)}), bf16[32,96,1024]{2,1,0:T(8,128)(2,1)}, u32[]{:S(2)}, u32[]{:S(2)}) async-start(bf16[32,96,1024]{2,1,0:T(8,128)(2,1)} %shard_map.68), calls=%async_computation | async-start | bytes 12582912 | tf_op jit(solution)/shard_map/all_to_all | solution.py:244
  15.0 0.0 copy-start
  15.0 3.6 %slice.23 = bf16[32,40,1024]{2,1,0:T(8,128)(2,1)} slice(bf16[32,128,1024]{2,1,0:T(8,128)(2,1)} %bitcast.22), slice={[0:32], [88:128], [0:1024]} | slice | bytes 5242880 | tf_op jit(solution)/shard_map/slice | solution.py:239
  18.6 0.0 copy-done
  18.6 0.5 multiply_reduce_fusion.1
  19.1 0.1 constant_dynamic-slice_fusion
  19.2 5.1 %multiply_reduce_fusion = f32[4096]{0:T(1024)S(1)} fusion(bf16[4096,1024]{1,0:T(8,128)(2,1)} %param.5), kind=kLoop, calls=%fused_computation | loop fusion | flops 12578816 | bytes 8404992 | tf_op jit(solution)/shard_map/reduce_sum | solution.py:235
  24.3 0.0 copy-start.4
  24.3 68.5 %all-to-all-done = bf16[32,96,1024]{2,1,0:T(8,128)(2,1)} async-done(((bf16[32,96,1024]{2,1,0:T(8,128)(2,1)}), bf16[32,96,1024]{2,1,0:T(8,128)(2,1)}, u32[]{:S(2)}, u32[]{:S(2)}) %all-to-all-start) | async-done | bytes 6291488 | tf_op jit(solution)/shard_map/all_to_all | solution.py:244
  92.8 4.2 %all-to-all-start.1 = ((bf16[32,40,1024]{2,1,0:T(8,128)(2,1)}), bf16[32,40,1024]{2,1,0:T(8,128)(2,1)S(1)}, u32[]{:S(2)}, u32[]{:S(2)}) async-start(bf16[32,40,1024]{2,1,0:T(8,128)(2,1)} %slice.23), calls=%async_computation.1 | async-start | bytes 5242880 | tf_op jit(solution)/shard_map/all_to_all | solution.py:244
  97.1 1.0 copy.10.refs_3_.refs_4_
  98.1 0.9 slice_convert_fusion
  99.0 0.1 slice.22
  99.1 0.7 reshape.68.refs_1_
  99.8 0.0 copy-done.4
  99.8 0.7 reshape.71.refs_0_
  100.4 20.3 %shard_map.69 = (f32[1,3072]{1,0:T(1,128)}, f32[1024,1024]{1,0:T(8,128)}, f32[1024,128]{1,0:T(8,128)}) custom-call(s32[1,3072]{1,0:T(1,128)} %reshape.71.refs_0_, bf16[3072,1024]{1,0:T(8,128)(2,1)} %bitcast.8.refs_1_, bf16[1024,1024]{1,0:T(8,128)(2,1)} %bitcast.23, f32[1024,1]{1,0:T(8,128)} %copy.10.refs_3_.refs_4_), custom_call_target="tpu_custom_call" | custom-call | flops 12884901888 | bytes 12582912 | tf_op jit(solution)/shard_map/pallas_call | solution.py:202
  120.7 12.3 %all-to-all-done.1 = bf16[32,40,1024]{2,1,0:T(8,128)(2,1)S(1)} async-done(((bf16[32,40,1024]{2,1,0:T(8,128)(2,1)}), bf16[32,40,1024]{2,1,0:T(8,128)(2,1)S(1)}, u32[]{:S(2)}, u32[]{:S(2)}) %all-to-all-start.1) | async-done | bytes 2621472 | tf_op jit(solution)/shard_map/all_to_all | solution.py:244
  133.0 0.0 copy-start.1
  133.0 1.5 copy-done.1
  134.5 0.0 copy-start.2
  134.5 0.0 copy-start.3
  134.5 11.5 %shard_map.70 = (f32[1,1280]{1,0:T(1,128)}, f32[1024,256]{1,0:T(8,128)}, s16[1088,256]{1,0:T(8,128)(2,1)}, s16[1088,256]{1,0:T(8,128)(2,1)}, s16[1088,256]{1,0:T(8,128)(2,1)}, /*index=5*/s16[64,256]{1,0:T(8,128)(2,1)}) custom-call(s32[1]{0:T(128)} %bitcast.refs_0_, s32[1,1280]{1,0:T(1,128)} %reshape.68.refs_1_, bf16[1280,1024]{1,0:T(8,128)(2,1)} %bitcast.26, ...), custom_call_target="tpu_custom_call" | custom-call | flops 5368709120 | bytes 8912896 | tf_op jit(solution)/shard_map/pallas_call | solution.py:202
  146.0 1.6 collective-permute-start
  147.7 2.9 %collective-permute-start.1 = (s16[1088,256]{1,0:T(8,128)(2,1)}, s16[1088,256]{1,0:T(8,128)(2,1)S(1)}, u32[]{:S(2)}, u32[]{:S(2)}) collective-permute-start(s16[1088,256]{1,0:T(8,128)(2,1)} %get-tuple-element.23), channel_id=1, source_target_pairs={{0,2},{1,3},{2,0},{3,1},{4,6},{5,7},{6,4},{7,5},{8,10},{9,11},{10,... | collective-permute-start | bytes 1671176 | tf_op jit(solution)/shard_map/ppermute | solution.py:261
  150.6 1.4 collective-permute-start.2
  151.9 0.7 reduce.3
  152.6 0.1 reshape.75
  152.7 0.5 broadcast.24
  153.2 0.0 copy-done.2
  153.2 0.7 reduce.6
  153.9 0.1 reshape.74
  154.0 0.7 pad_maximum_fusion
  154.7 3.8 %all-to-all-start.2 = ((f32[32,1,128]{2,1,0:T(1,128)}), f32[32,1,128]{2,1,0:T(1,128)S(1)}, u32[]{:S(2)}, u32[]{:S(2)}) async-start(f32[32,1,128]{2,1,0:T(1,128)} %bitcast.11), calls=%async_computation.2 | async-start | bytes 32768 | tf_op jit(solution)/shard_map/all_to_all | solution.py:264
  158.5 1.3 convert_add_fusion.own_ref
  159.8 0.8 convert_element_type.25.home_ref
  160.6 5.2 %all-to-all-done.2 = f32[32,1,128]{2,1,0:T(1,128)S(1)} async-done(((f32[32,1,128]{2,1,0:T(1,128)}), f32[32,1,128]{2,1,0:T(1,128)S(1)}, u32[]{:S(2)}, u32[]{:S(2)}) %all-to-all-start.2) | async-done | bytes 16416 | tf_op jit(solution)/shard_map/all_to_all | solution.py:264
  165.8 0.0 copy-done.3
  165.8 0.7 multiply_bitcast_fusion
  166.5 0.0 collective-permute-done.refs_0_
  166.5 6.5 %collective-permute-done.1.refs_1_ = s16[1088,256]{1,0:T(8,128)(2,1)S(1)} collective-permute-done((s16[1088,256]{1,0:T(8,128)(2,1)}, s16[1088,256]{1,0:T(8,128)(2,1)S(1)}, u32[]{:S(2)}, u32[]{:S(2)}) %collective-permute-start.1) | collective-permute-done | bytes 557088 | tf_op jit(solution)/shard_map/ppermute | solution.py:261
  172.9 0.0 collective-permute-done.2.refs_2_
  172.9 3.0 %shard_map.71 = f32[1024,256]{1,0:T(8,128)} custom-call(f32[1024,256]{1,0:T(8,128)S(1)} %convert_add_fusion.own_ref, f32[64,256]{1,0:T(8,128)S(1)} %convert_element_type.25.home_ref, s16[1088,256]{1,0:T(8,128)(2,1)S(1)} %collective-permute-done.refs_0_, s16[1088,256]{1,0:T(8,128)(2,1)S(1)} %collective-permute-done.1.refs_1_, ...), custom_call_target="tpu_custom_call" | custom-call | tf_op jit(solution)/shard_map/pallas_call | solution.py:130
  (3 shorter events, 0.0 us)
Async XLA Ops:
  6.6 86.2 %all-to-all-start = ((bf16[32,96,1024]{2,1,0:T(8,128)(2,1)}), bf16[32,96,1024]{2,1,0:T(8,128)(2,1)}, u32[]{:S(2)}, u32[]{:S(2)}) async-start(bf16[32,96,1024]{2,1,0:T(8,128)(2,1)} %shard_map.68), calls=%async_computation | async-start | bytes 12582912 | tf_op jit(solution)/shard_map/all_to_all | solution.py:244
  15.0 3.6 %copy-start = (bf16[4,256,1024]{2,1,0:T(8,128)(2,1)S(1)}, bf16[4,256,1024]{2,1,0:T(8,128)(2,1)}, u32[]{:S(2)}) copy-start(bf16[4,256,1024]{2,1,0:T(8,128)(2,1)} %param.9) | copy-start | bytes 6291460
  24.3 75.5 %copy-start.4 = (pred[96]{0:T(512)(128)(4,1)S(1)}, pred[96]{0:T(512)(128)(4,1)}, u32[]{:S(2)}) copy-start(pred[96]{0:T(512)(128)(4,1)} %constant.8.clone.1) | copy-start | bytes 292
  92.8 40.1 %all-to-all-start.1 = ((bf16[32,40,1024]{2,1,0:T(8,128)(2,1)}), bf16[32,40,1024]{2,1,0:T(8,128)(2,1)S(1)}, u32[]{:S(2)}, u32[]{:S(2)}) async-start(bf16[32,40,1024]{2,1,0:T(8,128)(2,1)} %slice.23), calls=%async_computation.1 | async-start | bytes 5242880 | tf_op jit(solution)/shard_map/all_to_all | solution.py:244
  133.0 1.5 copy-start.1
  134.5 18.8 %copy-start.2 = (f32[1,3072]{1,0:T(1,128)S(1)}, f32[1,3072]{1,0:T(1,128)}, u32[]{:S(2)}) copy-start(f32[1,3072]{1,0:T(1,128)} %get-tuple-element.26) | copy-start | bytes 36868
  134.5 31.3 %copy-start.3 = (s32[1,32]{1,0:T(1,128)S(1)}, s32[1,32]{1,0:T(1,128)}, u32[]{:S(2)}) copy-start(s32[1,32]{1,0:T(1,128)} %used_ref.1) | copy-start | bytes 388
  146.0 20.4 %collective-permute-start = (s16[1088,256]{1,0:T(8,128)(2,1)}, s16[1088,256]{1,0:T(8,128)(2,1)S(1)}, u32[]{:S(2)}, u32[]{:S(2)}) collective-permute-start(s16[1088,256]{1,0:T(8,128)(2,1)} %get-tuple-element.22), channel_id=1, source_target_pairs={{0,1},{1,2},{2,3},{3,0},{4,5},{5,6},{6,7},{7,4},{8,9},{9,10},{10,1... | collective-permute-start | bytes 1671176 | tf_op jit(solution)/shard_map/ppermute | solution.py:262
  147.7 25.3 %collective-permute-start.1 = (s16[1088,256]{1,0:T(8,128)(2,1)}, s16[1088,256]{1,0:T(8,128)(2,1)S(1)}, u32[]{:S(2)}, u32[]{:S(2)}) collective-permute-start(s16[1088,256]{1,0:T(8,128)(2,1)} %get-tuple-element.23), channel_id=1, source_target_pairs={{0,2},{1,3},{2,0},{3,1},{4,6},{5,7},{6,4},{7,5},{8,10},{9,11},{10,... | collective-permute-start | bytes 1671176 | tf_op jit(solution)/shard_map/ppermute | solution.py:261
  150.6 22.4 %collective-permute-start.2 = (s16[1088,256]{1,0:T(8,128)(2,1)}, s16[1088,256]{1,0:T(8,128)(2,1)S(1)}, u32[]{:S(2)}, u32[]{:S(2)}) collective-permute-start(s16[1088,256]{1,0:T(8,128)(2,1)} %get-tuple-element.24), channel_id=1, source_target_pairs={{0,3},{1,0},{2,1},{3,2},{4,7},{5,4},{6,5},{7,6},{8,11},{9,8},{10,9... | collective-permute-start | bytes 1671176 | tf_op jit(solution)/shard_map/ppermute | solution.py:263
  154.7 11.1 %all-to-all-start.2 = ((f32[32,1,128]{2,1,0:T(1,128)}), f32[32,1,128]{2,1,0:T(1,128)S(1)}, u32[]{:S(2)}, u32[]{:S(2)}) async-start(f32[32,1,128]{2,1,0:T(1,128)} %bitcast.11), calls=%async_computation.2 | async-start | bytes 32768 | tf_op jit(solution)/shard_map/all_to_all | solution.py:264

commit v5 on v4

--- a/solution.py
+++ b/solution.py
@@ -113,14 +113,15 @@
     g = pl.program_id(0)
     rows = pl.ds(pl.multiple_of(g * each, each), each)
     marks = pl.ds(pl.multiple_of(m + g * 16, 16), 16)
+    notes = [home_ref[...]] + [f[marks, :].astype(jnp.int32).astype(jnp.float32) for f in far]
+    turned = jnp.concatenate(notes * 2, axis=0).T
     total = 1.0
     summed = own_ref[...]
     for k in range(4):
-        note = far[k - 1][marks, :].astype(jnp.int32).astype(jnp.float32) if k else home_ref[...]
-        turned = jnp.concatenate([note] * 8, axis=0).T
-        total = total + (turned[:, 0:1] + turned[:, 1:2] * (1.0 / fine)) * 0.25
+        at = 16 * k
+        total = total + (turned[:, at:at + 1] + turned[:, at + 1:at + 2] * (1.0 / fine)) * 0.25
         if k:
-            summed = summed + far[k - 1][rows, :].astype(jnp.int32).astype(jnp.float32) * step_of(turned[:, 2:3])
+            summed = summed + far[k - 1][rows, :].astype(jnp.int32).astype(jnp.float32) * step_of(turned[:, at + 2:at + 3])
     out_ref[...] = summed / total
 
 

time: 176 us -> 176 us (level)
  no operation moved by 1% of the time
where the time goes in v5:
time: 176 us
  waiting for transfers between devices  92.4 us (52%)
  Pallas kernels  40.5 us (23%)
  starting transfers between devices  22.3 us (13%)
  other arithmetic  11.3 us (6%)
  local copies, waits for them, and re-layouts  8.37 us (5%)
    all_to_all x2, waiting for transfers between devices, body(): lax.all_to_all(part, 'clu', split_axis=0, concat_axis=0, tiled=True)  80.8 us
    pallas_call x2, Pallas kernels, assign(): pl.pallas_call(functools.partial(assign_kernel, tile, parts, first, last)...  31.8 us
    all_to_all x2, starting transfers between devices, body(): lax.all_to_all(part, 'clu', split_axis=0, concat_axis=0, tiled=True)  12.6 us
    ppermute x1, waiting for transfers between devices, body(): got2 = lax.ppermute(far2, 'row', around(2, groups))  6.46 us
    pallas_call x1, Pallas kernels, pack(): pl.pallas_call(functools.partial(pack_kernel, clusters, cut), grid=(owner...  5.97 us
    all_to_all x1, waiting for transfers between devices, body(): lax.all_to_all(jnp.concatenate(gains, axis=1), 'clu', split_axis=0, conca...  5.17 us
    reduce_sum x1, other arithmetic, body(): row_squares = jnp.sum(blocks.astype(jnp.float32) ** 2, axis=2)  5.09 us
    all_to_all x1, starting transfers between devices, body(): lax.all_to_all(jnp.concatenate(gains, axis=1), 'clu', split_axis=0, conca...  3.83 us
  transfers between devices with their start and end apart: 6, of which 4 were waited for; matrix products, arithmetic and copies ran while one was open for 10% of the time, Pallas kernels for 12%

profile of v5, /device:TPU:0, one launch (start us, length us, event | category | flops | bytes accessed | tf_op | source)
XLA Modules:
  0.0 175.7 jit_solution(9621751601363039116)
XLA Ops:
  0.6 6.0 %shard_map.68 = bf16[32,96,1024]{2,1,0:T(8,128)(2,1)} custom-call(s32[32,128]{1,0:T(8,128)} %bitcast.33, s32[1,128]{1,0:T(1,128)} %bitcast.36, s32[1,32]{1,0:T(1,128)} %used_ref.1, bf16[32,128,1024]{2,1,0:T(8,128)(2,1)} %bitcast.21), custom_call_target="tpu_custom_call" | custom-call | tf_op jit(solution)/shard_map/pallas_call | solution.py:164
  6.6 8.4 %all-to-all-start = ((bf16[32,96,1024]{2,1,0:T(8,128)(2,1)}), bf16[32,96,1024]{2,1,0:T(8,128)(2,1)}, u32[]{:S(2)}, u32[]{:S(2)}) async-start(bf16[32,96,1024]{2,1,0:T(8,128)(2,1)} %shard_map.68), calls=%async_computation | async-start | bytes 12582912 | tf_op jit(solution)/shard_map/all_to_all | solution.py:245
  15.0 0.0 copy-start
  15.0 3.6 %slice.23 = bf16[32,40,1024]{2,1,0:T(8,128)(2,1)} slice(bf16[32,128,1024]{2,1,0:T(8,128)(2,1)} %bitcast.22), slice={[0:32], [88:128], [0:1024]} | slice | bytes 5242880 | tf_op jit(solution)/shard_map/slice | solution.py:240
  18.6 0.0 copy-done
  18.6 0.5 multiply_reduce_fusion.1
  19.1 0.1 constant_dynamic-slice_fusion
  19.2 5.1 %multiply_reduce_fusion = f32[4096]{0:T(1024)S(1)} fusion(bf16[4096,1024]{1,0:T(8,128)(2,1)} %param.5), kind=kLoop, calls=%fused_computation | loop fusion | flops 12578816 | bytes 8404992 | tf_op jit(solution)/shard_map/reduce_sum | solution.py:236
  24.3 0.0 copy-start.4
  24.3 68.5 %all-to-all-done = bf16[32,96,1024]{2,1,0:T(8,128)(2,1)} async-done(((bf16[32,96,1024]{2,1,0:T(8,128)(2,1)}), bf16[32,96,1024]{2,1,0:T(8,128)(2,1)}, u32[]{:S(2)}, u32[]{:S(2)}) %all-to-all-start) | async-done | bytes 6291488 | tf_op jit(solution)/shard_map/all_to_all | solution.py:245
  92.8 4.2 %all-to-all-start.1 = ((bf16[32,40,1024]{2,1,0:T(8,128)(2,1)}), bf16[32,40,1024]{2,1,0:T(8,128)(2,1)S(1)}, u32[]{:S(2)}, u32[]{:S(2)}) async-start(bf16[32,40,1024]{2,1,0:T(8,128)(2,1)} %slice.23), calls=%async_computation.1 | async-start | bytes 5242880 | tf_op jit(solution)/shard_map/all_to_all | solution.py:245
  97.1 1.0 copy.10.refs_3_.refs_4_
  98.1 0.9 slice_convert_fusion
  99.0 0.1 slice.22
  99.1 0.7 reshape.68.refs_1_
  99.8 0.0 copy-done.4
  99.8 0.7 reshape.71.refs_0_
  100.4 20.3 %shard_map.69 = (f32[1,3072]{1,0:T(1,128)}, f32[1024,1024]{1,0:T(8,128)}, f32[1024,128]{1,0:T(8,128)}) custom-call(s32[1,3072]{1,0:T(1,128)} %reshape.71.refs_0_, bf16[3072,1024]{1,0:T(8,128)(2,1)} %bitcast.8.refs_1_, bf16[1024,1024]{1,0:T(8,128)(2,1)} %bitcast.23, f32[1024,1]{1,0:T(8,128)} %copy.10.refs_3_.refs_4_), custom_call_target="tpu_custom_call" | custom-call | flops 12884901888 | bytes 12582912 | tf_op jit(solution)/shard_map/pallas_call | solution.py:203
  120.7 12.3 %all-to-all-done.1 = bf16[32,40,1024]{2,1,0:T(8,128)(2,1)S(1)} async-done(((bf16[32,40,1024]{2,1,0:T(8,128)(2,1)}), bf16[32,40,1024]{2,1,0:T(8,128)(2,1)S(1)}, u32[]{:S(2)}, u32[]{:S(2)}) %all-to-all-start.1) | async-done | bytes 2621472 | tf_op jit(solution)/shard_map/all_to_all | solution.py:245
  133.0 0.0 copy-start.1
  133.0 1.5 copy-done.1
  134.5 0.0 copy-start.2
  134.5 0.0 copy-start.3
  134.5 11.5 %shard_map.70 = (f32[1,1280]{1,0:T(1,128)}, f32[1024,256]{1,0:T(8,128)}, s16[1088,256]{1,0:T(8,128)(2,1)}, s16[1088,256]{1,0:T(8,128)(2,1)}, s16[1088,256]{1,0:T(8,128)(2,1)}, /*index=5*/s16[64,256]{1,0:T(8,128)(2,1)}) custom-call(s32[1]{0:T(128)} %bitcast.refs_0_, s32[1,1280]{1,0:T(1,128)} %reshape.68.refs_1_, bf16[1280,1024]{1,0:T(8,128)(2,1)} %bitcast.26, ...), custom_call_target="tpu_custom_call" | custom-call | flops 5368709120 | bytes 8912896 | tf_op jit(solution)/shard_map/pallas_call | solution.py:203
  146.0 1.6 collective-permute-start
  147.7 2.9 %collective-permute-start.1 = (s16[1088,256]{1,0:T(8,128)(2,1)}, s16[1088,256]{1,0:T(8,128)(2,1)S(1)}, u32[]{:S(2)}, u32[]{:S(2)}) collective-permute-start(s16[1088,256]{1,0:T(8,128)(2,1)} %get-tuple-element.23), channel_id=1, source_target_pairs={{0,2},{1,3},{2,0},{3,1},{4,6},{5,7},{6,4},{7,5},{8,10},{9,11},{10,... | collective-permute-start | bytes 1671176 | tf_op jit(solution)/shard_map/ppermute | solution.py:262
  150.6 1.4 collective-permute-start.2
  151.9 0.7 reduce.3
  152.6 0.1 reshape.75
  152.7 0.5 broadcast.24
  153.2 0.0 copy-done.2
  153.2 0.7 reduce.6
  153.9 0.1 reshape.74
  154.0 0.7 pad_maximum_fusion
  154.7 3.8 %all-to-all-start.2 = ((f32[32,1,128]{2,1,0:T(1,128)}), f32[32,1,128]{2,1,0:T(1,128)S(1)}, u32[]{:S(2)}, u32[]{:S(2)}) async-start(f32[32,1,128]{2,1,0:T(1,128)} %bitcast.11), calls=%async_computation.2 | async-start | bytes 32768 | tf_op jit(solution)/shard_map/all_to_all | solution.py:265
  158.5 1.3 convert_add_fusion.own_ref
  159.8 0.8 convert_element_type.25.home_ref
  160.6 5.2 %all-to-all-done.2 = f32[32,1,128]{2,1,0:T(1,128)S(1)} async-done(((f32[32,1,128]{2,1,0:T(1,128)}), f32[32,1,128]{2,1,0:T(1,128)S(1)}, u32[]{:S(2)}, u32[]{:S(2)}) %all-to-all-start.2) | async-done | bytes 16416 | tf_op jit(solution)/shard_map/all_to_all | solution.py:265
  165.8 0.0 copy-done.3
  165.8 0.7 multiply_bitcast_fusion
  166.5 0.0 collective-permute-done.refs_0_
  166.5 6.5 %collective-permute-done.1.refs_1_ = s16[1088,256]{1,0:T(8,128)(2,1)S(1)} collective-permute-done((s16[1088,256]{1,0:T(8,128)(2,1)}, s16[1088,256]{1,0:T(8,128)(2,1)S(1)}, u32[]{:S(2)}, u32[]{:S(2)}) %collective-permute-start.1) | collective-permute-done | bytes 557088 | tf_op jit(solution)/shard_map/ppermute | solution.py:262
  172.9 0.0 collective-permute-done.2.refs_2_
  172.9 2.7 %shard_map.71 = f32[1024,256]{1,0:T(8,128)} custom-call(f32[1024,256]{1,0:T(8,128)S(1)} %convert_add_fusion.own_ref, f32[64,256]{1,0:T(8,128)S(1)} %convert_element_type.25.home_ref, s16[1088,256]{1,0:T(8,128)(2,1)S(1)} %collective-permute-done.refs_0_, s16[1088,256]{1,0:T(8,128)(2,1)S(1)} %collective-permute-done.1.refs_1_, ...), custom_call_target="tpu_custom_call" | custom-call | tf_op jit(solution)/shard_map/pallas_call | solution.py:131
  (3 shorter events, 0.0 us)
Async XLA Ops:
  6.6 86.2 %all-to-all-start = ((bf16[32,96,1024]{2,1,0:T(8,128)(2,1)}), bf16[32,96,1024]{2,1,0:T(8,128)(2,1)}, u32[]{:S(2)}, u32[]{:S(2)}) async-start(bf16[32,96,1024]{2,1,0:T(8,128)(2,1)} %shard_map.68), calls=%async_computation | async-start | bytes 12582912 | tf_op jit(solution)/shard_map/all_to_all | solution.py:245
  15.0 3.6 %copy-start = (bf16[4,256,1024]{2,1,0:T(8,128)(2,1)S(1)}, bf16[4,256,1024]{2,1,0:T(8,128)(2,1)}, u32[]{:S(2)}) copy-start(bf16[4,256,1024]{2,1,0:T(8,128)(2,1)} %param.9) | copy-start | bytes 6291460
  24.3 75.5 %copy-start.4 = (pred[96]{0:T(512)(128)(4,1)S(1)}, pred[96]{0:T(512)(128)(4,1)}, u32[]{:S(2)}) copy-start(pred[96]{0:T(512)(128)(4,1)} %constant.8.clone.1) | copy-start | bytes 292
  92.8 40.1 %all-to-all-start.1 = ((bf16[32,40,1024]{2,1,0:T(8,128)(2,1)}), bf16[32,40,1024]{2,1,0:T(8,128)(2,1)S(1)}, u32[]{:S(2)}, u32[]{:S(2)}) async-start(bf16[32,40,1024]{2,1,0:T(8,128)(2,1)} %slice.23), calls=%async_computation.1 | async-start | bytes 5242880 | tf_op jit(solution)/shard_map/all_to_all | solution.py:245
  133.0 1.5 copy-start.1
  134.5 18.8 %copy-start.2 = (f32[1,3072]{1,0:T(1,128)S(1)}, f32[1,3072]{1,0:T(1,128)}, u32[]{:S(2)}) copy-start(f32[1,3072]{1,0:T(1,128)} %get-tuple-element.26) | copy-start | bytes 36868
  134.5 31.3 %copy-start.3 = (s32[1,32]{1,0:T(1,128)S(1)}, s32[1,32]{1,0:T(1,128)}, u32[]{:S(2)}) copy-start(s32[1,32]{1,0:T(1,128)} %used_ref.1) | copy-start | bytes 388
  146.0 20.4 %collective-permute-start = (s16[1088,256]{1,0:T(8,128)(2,1)}, s16[1088,256]{1,0:T(8,128)(2,1)S(1)}, u32[]{:S(2)}, u32[]{:S(2)}) collective-permute-start(s16[1088,256]{1,0:T(8,128)(2,1)} %get-tuple-element.22), channel_id=1, source_target_pairs={{0,1},{1,2},{2,3},{3,0},{4,5},{5,6},{6,7},{7,4},{8,9},{9,10},{10,1... | collective-permute-start | bytes 1671176 | tf_op jit(solution)/shard_map/ppermute | solution.py:263
  147.7 25.3 %collective-permute-start.1 = (s16[1088,256]{1,0:T(8,128)(2,1)}, s16[1088,256]{1,0:T(8,128)(2,1)S(1)}, u32[]{:S(2)}, u32[]{:S(2)}) collective-permute-start(s16[1088,256]{1,0:T(8,128)(2,1)} %get-tuple-element.23), channel_id=1, source_target_pairs={{0,2},{1,3},{2,0},{3,1},{4,6},{5,7},{6,4},{7,5},{8,10},{9,11},{10,... | collective-permute-start | bytes 1671176 | tf_op jit(solution)/shard_map/ppermute | solution.py:262
  150.6 22.4 %collective-permute-start.2 = (s16[1088,256]{1,0:T(8,128)(2,1)}, s16[1088,256]{1,0:T(8,128)(2,1)S(1)}, u32[]{:S(2)}, u32[]{:S(2)}) collective-permute-start(s16[1088,256]{1,0:T(8,128)(2,1)} %get-tuple-element.24), channel_id=1, source_target_pairs={{0,3},{1,0},{2,1},{3,2},{4,7},{5,4},{6,5},{7,6},{8,11},{9,8},{10,9... | collective-permute-start | bytes 1671176 | tf_op jit(solution)/shard_map/ppermute | solution.py:264
  154.7 11.1 %all-to-all-start.2 = ((f32[32,1,128]{2,1,0:T(1,128)}), f32[32,1,128]{2,1,0:T(1,128)S(1)}, u32[]{:S(2)}, u32[]{:S(2)}) async-start(f32[32,1,128]{2,1,0:T(1,128)} %bitcast.11), calls=%async_computation.2 | async-start | bytes 32768 | tf_op jit(solution)/shard_map/all_to_all | solution.py:265
